TPU v7x, 256 devices: a whole 4x4x8 slice. The times are simulated.
256 devices in a mesh: train: 16 (over z_hi, y, core), feat: 16 (over x, z_lo).
Axes of the slice: x: 4, y: 4, z: 8 (z_hi: 2, z_lo: 4; z = z_hi * 4 + z_lo), core: 2. Of those that a mesh axis runs over, the one named last changes fastest.
Arguments:
- queries: bfloat16 [2048, 65536], P('train', 'feat'), may hold values from -6 to 6
- group_order: int32 [16, 128], P('train'), may hold values from 0 to 127, each once within a row
- train_features: bfloat16 [16384, 65536], P('train', 'feat'), may hold values from -0.0234375 to 0.0234375
- doc_ids: int32 [16, 1024], P('train'), may hold values from 0 to 255, never falling along the last dimension, each value on 1 to 8 neighbouring positions
- sketch_rows: bfloat16 [1024, 65536], P('train', 'feat'), may hold values from -6 to 6
- sketch_scale: float32 [1024], replicated, may hold values from 0.5 to 2
- sketch_values: float32 [1024], replicated, may hold values from 0.25 to 8
Outputs:
- attribution: float32 [4096, 4, 128], P(('train', 'feat'))
All inputs are finite; a program needn't handle non-finite values.
Results may differ from a plain program's by a relative error of at most 0.0034.
Values may be sent and summed in bfloat16 or wider, within the bound.
No kernel may reach another device: no remote copies, remote signals or barrier semaphores. Data moves between devices by JAX's collectives and lax.ppermute only.
A program may use at most 64 MiB of HBM per device.

v0:
```python
import math

import jax
import jax.numpy as jnp
from jax import lax
from jax.sharding import PartitionSpec as P

F = 65536
STEPS = 4
DOC_DEV = 256


def from_behind(value, axis, steps):
    count = lax.axis_size(axis)
    pairs = [(source, (source + steps) % count) for source in range(count)]
    return lax.ppermute(value, axis, pairs)


def scale_sketch(sketch_rows, sketch_scale):
    factor = 1.0 / math.sqrt(F)
    return (sketch_rows.astype(jnp.float32) * (sketch_scale[:, None] * factor)).astype(jnp.bfloat16)


def per_device(
    queries, group_order, train_features, doc_ids, sketch_rows, sketch_scale, sketch_values
):
    all_rows = lax.all_gather(sketch_rows, "train", axis=0, tiled=True)
    sketch = scale_sketch(all_rows, sketch_scale)
    weight = sketch_values * sketch_values / (1.0 + sketch_values * sketch_values)
    query_block = jnp.take(queries, group_order[0], axis=0)
    partial_value = jnp.dot(query_block, sketch.T, preferred_element_type=jnp.float32)
    coef = lax.psum(partial_value, "feat")
    weighted = (coef * weight[None, :]).astype(jnp.bfloat16)
    correction = jnp.dot(weighted, sketch, preferred_element_type=jnp.float32)
    conditioned = (query_block.astype(jnp.float32) - correction).astype(jnp.bfloat16)
    onehot = (doc_ids[0][None, :] == jnp.arange(DOC_DEV, dtype=jnp.int32)[:, None]).astype(
        jnp.float32
    )
    step_terms = []
    visiting = conditioned
    for offset in range(STEPS):
        if offset > 0:
            visiting = from_behind(visiting, "train", 1)
        row_scores = jnp.dot(train_features, visiting.T, preferred_element_type=jnp.float32)
        step_terms.append(jnp.dot(onehot, row_scores, precision=lax.Precision.HIGHEST))
    summed = [
        lax.psum_scatter(term_scores, "feat", scatter_dimension=0, tiled=True)
        for term_scores in step_terms
    ]
    return jnp.stack(summed, axis=1)


def solution(mesh):
    in_specs = (
        P("train", "feat"),
        P("train", None),
        P("train", "feat"),
        P("train", None),
        P("train", "feat"),
        P(),
        P(),
    )
    out_specs = P(("train", "feat"), None, None)
    return jax.shard_map(
        per_device, mesh=mesh, in_specs=in_specs, out_specs=out_specs, check_vma=False
    )
```

profile of v0, /device:TPU:8, one launch (start us, length us, event | category | flops | bytes accessed | tf_op | source)
XLA Modules:
  0.0 675.1 jit_solution(18113173284934439879)
XLA Ops:
  6.5 0.0 copy-start
  6.5 0.0 copy-start.4
  6.5 0.0 copy-start.2
  6.5 0.0 all-gather.2.cloned.1.call-start
  6.5 0.7 all-gather.2.cloned.1.call-update
  7.3 0.0 all-reduce.2.cloned.1.call-start
  7.3 0.7 fusion.11
  8.0 0.0 copy-done
  8.0 1.2 gather_fusion
  9.2 0.0 copy-done.4
  9.2 0.0 copy-start.3
  9.2 0.0 copy-done.2
  9.2 110.8 %all-gather.2.cloned.1.call-done = bf16[1024,4096]{1,0:T(8,128)(2,1)} async-done(((bf16[64,4096]{1,0:T(8,128)(2,1)}), bf16[1024,4096]{1,0:T(8,128)(2,1)}) %all-gather.2.cloned.1.call-update) | async-done | bytes 8388624 | tf_op jit(solution)/shard_map/all_gather | solution.py:27
  120.0 7.2 %fusion.1 = f32[128,1024]{1,0:T(8,128)} fusion(bf16[1024,4096]{1,0:T(8,128)(2,1)} %all-gather.2.cloned.1.call-done, f32[1024]{0:T(1024)S(1)} %broadcast_multiply_fusion, bf16[128,4096]{1,0:T(8,128)(2,1)S(1)} %gather_fusion, pred[128]{0:T(512)(128)(4,1)S(1)} %compare_and_fusion), kind=kOutput, calls=%fused_computation.4 | convolution fusion | flops 1086849024 | bytes 9965696 | tf_op jit(solution)/shard_map/dot_general | solution.py:31
  127.2 0.0 all-reduce.2.cloned.1.call-update
  127.3 0.0 reduce-scatter.5.cloned.1.call-start
  127.3 0.0 copy-done.3
  127.3 157.4 %all-reduce.2.cloned.1.call-done = f32[128,1024]{1,0:T(8,128)} async-done(((f32[128,1024]{1,0:T(8,128)}), f32[128,1024]{1,0:T(8,128)}) %all-reduce.2.cloned.1.call-update) | async-done | bytes 524304 | tf_op jit(solution)/shard_map/psum | solution.py:32
  284.8 5.8 fusion
  290.5 0.0 copy-start.1
  290.6 0.1 collective-permute-start
  290.6 14.2 %collective-permute-done = bf16[128,4096]{1,0:T(8,128)(2,1)S(1)} collective-permute-done((bf16[128,4096]{1,0:T(8,128)(2,1)S(1)}, bf16[128,4096]{1,0:T(8,128)(2,1)S(1)}, u32[]{:S(2)}, u32[]{:S(2)}) %collective-permute-start) | collective-permute-done | bytes 1048608 | tf_op jit(solution)/shard_map/ppermute | solution.py:16
  304.9 0.0 collective-permute-start.1
  304.9 6.3 fusion.13
  311.2 0.0 copy-done.1
  311.2 1.3 fusion.5
  312.5 0.0 reduce-scatter.5.cloned.1.call-update
  312.6 0.0 reduce-scatter.7.cloned.1.call-start
  312.6 6.3 fusion.14
  318.9 0.1 collective-permute-done.1
  319.1 1.7 collective-permute-start.2
  320.8 1.3 fusion.4
  322.2 0.0 reduce-scatter.7.cloned.1.call-update
  322.2 0.0 reduce-scatter.9.cloned.1.call-start
  322.2 6.3 fusion.15
  328.6 1.3 fusion.3
  329.9 0.0 reduce-scatter.9.cloned.1.call-update
  329.9 0.0 reduce-scatter.11.cloned.1.call-start
  330.0 7.6 %collective-permute-done.2 = bf16[128,4096]{1,0:T(8,128)(2,1)S(1)} collective-permute-done((bf16[128,4096]{1,0:T(8,128)(2,1)S(1)}, bf16[128,4096]{1,0:T(8,128)(2,1)S(1)}, u32[]{:S(2)}, u32[]{:S(2)}) %collective-permute-start.2) | collective-permute-done | bytes 1048608 | tf_op jit(solution)/shard_map/ppermute | solution.py:16
  337.5 6.3 fusion.16
  343.9 1.3 fusion.2
  345.2 0.0 reduce-scatter.11.cloned.1.call-update
  345.2 67.7 %reduce-scatter.5.cloned.1.call-done = f32[16,128]{1,0:T(8,128)} async-done(((f32[256,128]{1,0:T(8,128)}), f32[16,128]{1,0:T(8,128)}) %reduce-scatter.5.cloned.1.call-update) | async-done | bytes 8208 | tf_op jit(solution)/shard_map/reduce_scatter | solution.py:47
  412.9 89.3 %reduce-scatter.7.cloned.1.call-done = f32[16,128]{1,0:T(8,128)} async-done(((f32[256,128]{1,0:T(8,128)}), f32[16,128]{1,0:T(8,128)}) %reduce-scatter.7.cloned.1.call-update) | async-done | bytes 8208 | tf_op jit(solution)/shard_map/reduce_scatter | solution.py:47
  502.2 82.4 %reduce-scatter.9.cloned.1.call-done = f32[16,128]{1,0:T(8,128)} async-done(((f32[256,128]{1,0:T(8,128)}), f32[16,128]{1,0:T(8,128)}) %reduce-scatter.9.cloned.1.call-update) | async-done | bytes 8208 | tf_op jit(solution)/shard_map/reduce_scatter | solution.py:47
  584.6 82.3 %reduce-scatter.11.cloned.1.call-done = f32[16,128]{1,0:T(8,128)} async-done(((f32[256,128]{1,0:T(8,128)}), f32[16,128]{1,0:T(8,128)}) %reduce-scatter.11.cloned.1.call-update) | async-done | bytes 8208 | tf_op jit(solution)/shard_map/reduce_scatter | solution.py:47
  666.9 0.7 pad_maximum_fusion
  667.7 0.6 copy.8
  (4 shorter events, 0.0 us)
Async XLA Ops:
  6.5 1.4 copy-start
  6.5 2.6 copy-start.4
  6.5 2.7 copy-start.2
  6.5 113.5 %all-gather.2.cloned.1.call-start = ((), (), s32[]{:S(2)}) async-start(), calls=%async_computation.4 | async-start | bytes 8912896 | tf_op jit(solution)/shard_map/all_gather | solution.py:27
  7.3 277.5 %all-reduce.2.cloned.1.call-start = ((), (), s32[]{:S(2)}) async-start(), calls=%async_computation.5 | async-start | bytes 1048576 | tf_op jit(solution)/shard_map/psum | solution.py:32
  9.2 118.1 %copy-start.3 = (f32[1024]{0:T(1024)S(1)}, f32[1024]{0:T(1024)}, u32[]{:S(2)}) copy-start(f32[1024]{0:T(1024)} %param.13) | copy-start | bytes 12292
  127.3 285.7 %reduce-scatter.5.cloned.1.call-start = ((), (), s32[]{:S(2)}) async-start(), calls=%async_computation.6 | async-start | bytes 139264 | tf_op jit(solution)/shard_map/reduce_scatter | solution.py:47
  290.5 20.7 %copy-start.1 = (s32[1,1024]{1,0:T(1,128)S(1)}, s32[1,1024]{1,0:T(1,128)}, u32[]{:S(2)}) copy-start(s32[1,1024]{1,0:T(1,128)} %param.10) | copy-start | bytes 12292
  290.6 14.3 %collective-permute-start = (bf16[128,4096]{1,0:T(8,128)(2,1)S(1)}, bf16[128,4096]{1,0:T(8,128)(2,1)S(1)}, u32[]{:S(2)}, u32[]{:S(2)}) collective-permute-start(bf16[128,4096]{1,0:T(8,128)(2,1)S(1)} %fusion), channel_id=1, source_target_pairs={{0,16},{16,32},{32,48},{48,64},{64,80},{80,96},{96,112},{112,128},... | collective-permute-start | bytes 3145736 | tf_op jit(solution)/shard_map/ppermute | solution.py:16
  304.9 14.2 %collective-permute-start.1 = (bf16[128,4096]{1,0:T(8,128)(2,1)S(1)}, bf16[128,4096]{1,0:T(8,128)(2,1)S(1)}, u32[]{:S(2)}, u32[]{:S(2)}) collective-permute-start(bf16[128,4096]{1,0:T(8,128)(2,1)S(1)} %collective-permute-done), channel_id=1, source_target_pairs={{0,16},{16,32},{32,48},{48,64},{64,80},{80,96},{96,112},{112,128},... | collective-permute-start | bytes 3145736 | tf_op jit(solution)/shard_map/ppermute | solution.py:16
  312.6 189.6 %reduce-scatter.7.cloned.1.call-start = ((), (), s32[]{:S(2)}) async-start(), calls=%async_computation.7 | async-start | bytes 139264 | tf_op jit(solution)/shard_map/reduce_scatter | solution.py:47
  319.1 18.4 %collective-permute-start.2 = (bf16[128,4096]{1,0:T(8,128)(2,1)S(1)}, bf16[128,4096]{1,0:T(8,128)(2,1)S(1)}, u32[]{:S(2)}, u32[]{:S(2)}) collective-permute-start(bf16[128,4096]{1,0:T(8,128)(2,1)S(1)} %collective-permute-done.1), channel_id=1, source_target_pairs={{0,16},{16,32},{32,48},{48,64},{64,80},{80,96},{96,112},{112,128},... | collective-permute-start | bytes 3145736 | tf_op jit(solution)/shard_map/ppermute | solution.py:16
  322.2 262.4 %reduce-scatter.9.cloned.1.call-start = ((), (), s32[]{:S(2)}) async-start(), calls=%async_computation.8 | async-start | bytes 139264 | tf_op jit(solution)/shard_map/reduce_scatter | solution.py:47
  329.9 337.0 %reduce-scatter.11.cloned.1.call-start = ((), (), s32[]{:S(2)}) async-start(), calls=%async_computation.9 | async-start | bytes 139264 | tf_op jit(solution)/shard_map/reduce_scatter | solution.py:47
Sparse Core Ops, SparseCore 0:
  10.1 109.8 all-gather.1
  127.4 157.3 all-reduce.1
  312.7 100.2 reduce-scatter.4
  415.3 86.8 reduce-scatter.6
  504.7 79.8 reduce-scatter.8
  587.0 79.9 reduce-scatter.10
where the time goes:
time: 675 us
  waiting for transfers between devices  613 us (91%)
  matrix products  43.6 us (6%)
  between operations  13.6 us (2%)
    reduce_scatter x4, waiting for transfers between devices, per_device(): lax.psum_scatter(term_scores, 'feat', scatter_dimension=0, tiled=True)  322 us
    psum x1, waiting for transfers between devices, per_device(): coef = lax.psum(partial_value, 'feat')  157 us
    all_gather x1, waiting for transfers between devices, per_device(): all_rows = lax.all_gather(sketch_rows, 'train', axis=0, tiled=True)  111 us
    dot_general x4, matrix products, per_device(): jnp.dot(train_features, visiting.T, preferred_element_type=jnp.float32)  25.3 us
    ppermute x3, waiting for transfers between devices, from_behind(): return lax.ppermute(value, axis, pairs)  21.9 us
  transfers between devices with their start and end apart: 9, of which 9 were waited for; matrix products, arithmetic and copies ran while one was open for 5% of the time, Pallas kernels for 0%

commit v1 on v0

v1 whole, which is shorter than its diff:
```python
import functools
import math

import jax
import jax.numpy as jnp
from jax import lax
from jax.experimental import pallas as pl
from jax.experimental.pallas import tpu as pltpu
from jax.sharding import PartitionSpec as P

DOC_DEV = 256
BOTH = ("train", "feat")


def pairs_of(move, keep=lambda z, y, c, x, l: True):
    def index(z, y, c, x, l):
        return ((z * 4 + y) * 2 + c) * 16 + x * 4 + l

    out = []
    for z in range(2):
        for y in range(4):
            for c in range(2):
                for x in range(4):
                    for l in range(4):
                        if keep(z, y, c, x, l):
                            out.append((index(z, y, c, x, l), index(*move(z, y, c, x, l))))
    return out


def chip_up(steps, mirrored=False):
    def move(z, y, c, x, l):
        p = (z * 4 + y + steps) % 8
        return (p // 4, p % 4, c, x, 3 - l if mirrored and p // 4 != z else l)

    return move


CORE = pairs_of(lambda z, y, c, x, l: (z, y, 1 - c, x, l))
Y_UP = pairs_of(lambda z, y, c, x, l: (z, (y + 1) % 4, c, x, l))
Y_DOWN = pairs_of(lambda z, y, c, x, l: (z, (y + 3) % 4, c, x, l))
Y_TWO = pairs_of(lambda z, y, c, x, l: (z, (y + 2) % 4, c, x, l))
Z_FLIP = pairs_of(lambda z, y, c, x, l: (1 - z, y, c, x, l))
COEF_UP = pairs_of(chip_up(1, mirrored=True))
COEF_UP2 = pairs_of(chip_up(2, mirrored=True))
ODD_UP = pairs_of(lambda z, y, c, x, l: (z, (y + 1) % 4, c, x, l), lambda z, y, c, x, l: c == 1)
CROSS = pairs_of(
    lambda z, y, c, x, l: (1 - z, y, c, x, l),
    lambda z, y, c, x, l: (y, c) in ((3, 0), (0, 1), (2, 1)),
)
EVEN_UP = pairs_of(
    lambda z, y, c, x, l: (z, (y + 1) % 4, c, x, l), lambda z, y, c, x, l: c == 0 and y != 3
)
ODD_AGAIN = pairs_of(
    lambda z, y, c, x, l: (z, (y + 1) % 4, c, x, l), lambda z, y, c, x, l: c == 1 and y in (1, 2)
)
CROSSED_ON = pairs_of(
    lambda z, y, c, x, l: (z, {3: 0, 0: 1, 2: 0}[y], c, x, l),
    lambda z, y, c, x, l: (y, c) in ((3, 0), (0, 1), (2, 1)),
)


def permute(value, pairs):
    return lax.ppermute(value, BOTH, pairs)


def hold_kernel(*refs):
    del refs


def hold(value, *after):
    return pl.pallas_call(
        hold_kernel,
        out_shape=jax.ShapeDtypeStruct(value.shape, value.dtype),
        in_specs=[pl.BlockSpec(memory_space=pl.ANY)] * (1 + len(after)),
        out_specs=pl.BlockSpec(memory_space=pl.ANY),
        input_output_aliases={0: 0},
        cost_estimate=QUICK,
        name="hold",
    )(value, *after)


QUICK = pl.CostEstimate(flops=0, bytes_accessed=0, transcendentals=0)
VMEM = pl.BlockSpec(memory_space=pltpu.VMEM)
ANY = pl.BlockSpec(memory_space=pl.ANY)
PARAMS = pltpu.CompilerParams(vmem_limit_bytes=20 * 1024 * 1024)


def dot_t(a, b):
    return lax.dot_general(a, b, (((1,), (1,)), ((), ())), preferred_element_type=jnp.float32)


def stretches(width):
    wide = min(1024, width)
    return [slice(k, k + wide) for k in range(0, width, wide)]


def pick_kernel(order_ref, rows_ref, *refs):
    out_ref = refs[-1]
    n, width = out_ref.shape
    slot = lax.broadcasted_iota(jnp.int32, (n, n), 0)
    put = (slot == order_ref[...]).astype(jnp.float32).astype(jnp.bfloat16)
    for k in stretches(width):
        out_ref[:, k] = lax.dot_general(
            put, rows_ref[:, k], (((0,), (0,)), ((), ())), preferred_element_type=jnp.float32
        ).astype(jnp.bfloat16)


def pick_rows(order, rows, *after):
    return pl.pallas_call(
        pick_kernel,
        out_shape=jax.ShapeDtypeStruct(rows.shape, jnp.bfloat16),
        in_specs=[VMEM, VMEM] + [ANY] * len(after),
        out_specs=VMEM,
        compiler_params=PARAMS,
        cost_estimate=QUICK,
        name="pick_rows",
    )(order, rows, *after)


def docs_kernel(ids_ref, rows_ref, *refs):
    out_ref, held, sems = refs[-3:]
    parts = stretches(held.shape[1])
    copies = [
        pltpu.make_async_copy(rows_ref.at[:, k], held.at[:, k], sems.at[j])
        for j, k in enumerate(parts)
    ]
    for copy in copies:
        copy.start()
    doc = lax.broadcasted_iota(jnp.int32, (DOC_DEV, held.shape[0]), 0)
    member = (doc == ids_ref[...]).astype(jnp.float32).astype(jnp.bfloat16)
    for copy, k in zip(copies, parts):
        copy.wait()
        out_ref[:, k] = jnp.dot(
            member, held[:, k], preferred_element_type=jnp.float32
        ).astype(jnp.bfloat16)


def sum_docs(ids, rows, *after):
    width = rows.shape[1]
    return pl.pallas_call(
        docs_kernel,
        out_shape=jax.ShapeDtypeStruct((DOC_DEV, width), jnp.bfloat16),
        in_specs=[VMEM, ANY] + [ANY] * len(after),
        out_specs=VMEM,
        scratch_shapes=[
            pltpu.VMEM(rows.shape, jnp.bfloat16),
            pltpu.SemaphoreType.DMA((len(stretches(width)),)),
        ],
        compiler_params=PARAMS,
        cost_estimate=QUICK,
        name="sum_docs",
    )(ids, rows, *after)


def products_kernel(flag, order_ref, *refs):
    ins, out_ref = refs[:12], refs[-5]
    near, far, columns, sems = refs[-4:]
    places = []
    for place, group in ((near, ins[:4]), (far, ins[4:8]), (columns, ins[8:])):
        at = 0
        for ref in group:
            places.append(place.at[at : at + ref.shape[0]])
            at += ref.shape[0]
    parts = stretches(near.shape[1])
    copies = [
        [
            pltpu.make_async_copy(ref.at[:, k], place.at[:, k], sems.at[j, i])
            for i, (ref, place) in enumerate(zip(ins, places))
        ]
        for j, k in enumerate(parts)
    ]
    for part in copies:
        for copy in part:
            copy.start()
    totals = [None, None]
    for part, k in zip(copies, parts):
        for copy in part:
            copy.wait()
        for i, rows in enumerate((near, far)):
            value = dot_t(columns[:, k], rows[:, k])
            totals[i] = value if totals[i] is None else totals[i] + value
    for i, total in enumerate(totals):
        value = dot_t(order_ref[...], total.astype(jnp.bfloat16)).astype(jnp.bfloat16)
        value = value.reshape(16, 16, value.shape[1])

        @pl.when(flag[0] == i)
        def _():
            out_ref[:, :16, :] = value

        @pl.when(flag[0] != i)
        def _():
            out_ref[:, 16:, :] = value


def products(flag, order, near, far, others):
    width = near[0].shape[1]
    n_rows, n_cols = order.shape[0], sum(v.shape[0] for v in others)
    n = len(near) + len(far) + len(others)
    return pl.pallas_call(
        products_kernel,
        out_shape=jax.ShapeDtypeStruct((16, 2 * n_rows // 16, n_cols), jnp.bfloat16),
        in_specs=[pl.BlockSpec(memory_space=pltpu.SMEM), VMEM] + [ANY] * n,
        out_specs=VMEM,
        scratch_shapes=[
            pltpu.VMEM((n_rows, width), jnp.bfloat16),
            pltpu.VMEM((n_rows, width), jnp.bfloat16),
            pltpu.VMEM((n_cols, width), jnp.bfloat16),
            pltpu.SemaphoreType.DMA((len(stretches(width)), n)),
        ],
        compiler_params=pltpu.CompilerParams(vmem_limit_bytes=28 * 1024 * 1024),
        cost_estimate=QUICK,
        name="products",
    )(flag, order, *near, *far, *others)


def direct_kernel(flags, d_ref, do_ref, q_ref, up1, cross, even, odd, on, own_ref, other_ref):
    first, y = flags[0] == 1, flags[1]
    n = q_ref.shape[0]
    own = other = None
    for k in stretches(q_ref.shape[1]):
        block_2 = jnp.where(
            y == 0,
            jnp.where(first, on[:, k], cross[:, k]),
            jnp.where(first, even[:, k], up1[:, k]),
        )
        block_4 = jnp.where(y < 2, on[:, k], odd[:, k])
        blocks = jnp.concatenate([q_ref[:, k], block_2, block_4], axis=0)
        part, part_o = dot_t(d_ref[:, k], blocks[: 2 * n]), dot_t(do_ref[:, k], blocks)
        own = part if own is None else own + part
        other = part_o if other is None else other + part_o
    own_ref[...] = own
    other_ref[...] = other


def direct_products(flags, docs, docs_o, blocks):
    n = blocks[0].shape[0]
    return pl.pallas_call(
        direct_kernel,
        out_shape=[
            jax.ShapeDtypeStruct((DOC_DEV, 2 * n), jnp.float32),
            jax.ShapeDtypeStruct((DOC_DEV, 3 * n), jnp.float32),
        ],
        in_specs=[pl.BlockSpec(memory_space=pltpu.SMEM)] + [VMEM] * (2 + len(blocks)),
        out_specs=[VMEM, VMEM],
        compiler_params=PARAMS,
        cost_estimate=pl.CostEstimate(
            flops=50 * n * DOC_DEV * docs.shape[1],
            bytes_accessed=2 * (2 * DOC_DEV + 6 * n) * docs.shape[1],
            transcendentals=0,
        ),
        name="direct_products",
    )(flags, docs, docs_o, *blocks)


def reduce_rows(value, x, l):
    rows, n = value.shape
    parts = value.reshape(4, rows // 4, n)

    def part(i):
        return lax.dynamic_index_in_dim(parts, (x + i) % 4, 0, keepdims=False)

    total = part(0)
    for i in (2, 1, 3):
        total = total + permute(
            part(i), pairs_of(lambda z, y, c, xx, ll, i=i: (z, y, c, (xx + i) % 4, ll))
        )
    parts2 = total.reshape(4, rows // 16, n)

    def part2(i):
        return lax.dynamic_index_in_dim(parts2, (l + i) % 4, 0, keepdims=False)

    total = part2(0)
    for i in (2, 1, 3):
        total = total + permute(
            part2(i), pairs_of(lambda z, y, c, xx, ll, i=i: (z, y, c, xx, (ll + i) % 4))
        )
    return total


def per_device(
    queries, group_order, train_features, doc_ids, sketch_rows, sketch_scale, sketch_values
):
    qc, width = queries.shape
    bf16 = jnp.bfloat16
    t = lax.axis_index("train")
    f = lax.axis_index("feat")
    z, y, c = t // 8, (t // 2) % 4, t % 2
    x, l = f // 4, f % 4
    first = c == 0

    own = sketch_rows
    below, above = permute(own, Y_UP), permute(own, Y_DOWN)
    far_raw = permute(own, Z_FLIP)
    opposite = permute(above, Y_DOWN)
    near = [own, above, opposite, below]

    block = pick_rows(group_order, queries)
    up1 = permute(block, ODD_UP)
    block_o = permute(block, CORE)
    row = jnp.arange(256, dtype=jnp.int32)
    to_f, to_y, to_r = row // 16, (row // 4) % 4, row % 4
    to_slice = jnp.where(z == 0, to_f, to_f ^ 3)
    source = ((to_y - y) % 4) * 64 + to_slice * 4 + to_r
    order = (source[:, None] == row[None, :]).astype(bf16)
    far_own = hold(far_raw, below, opposite)
    far_below, far_above = permute(far_own, Y_UP), permute(far_own, Y_DOWN)
    far_opposite = permute(far_own, Y_TWO)
    far = [far_own, far_above, far_opposite, far_below]

    docs = sum_docs(doc_ids, train_features)
    docs_o = permute(docs, CORE)

    others = (block, docs, block_o, docs_o)

    bottom = y == 0
    cross = permute(hold(jnp.where(bottom, up1, block), far_own), CROSS)
    even_on = permute(hold(block, far_opposite), EVEN_UP)
    odd_on = permute(hold(up1, far_opposite), ODD_AGAIN)
    crossed = permute(hold(cross, far_opposite), CROSSED_ON)

    sent = products(z.reshape(1), order, near, far, others)
    got = lax.all_to_all(sent, "feat", 0, 0)
    summed = jnp.sum(got.astype(jnp.float32), axis=0)

    slab = jnp.arange(32, dtype=jnp.int32)
    held = (slab // 4) * 128 + c * 64 + jnp.where(z == 0, f, f ^ 3) * 4 + slab % 4
    scale = sketch_scale[held] * (1.0 / math.sqrt(16 * width))
    values = sketch_values[held]
    factor = scale * scale * (values * values / (1.0 + values * values))
    n = qc + DOC_DEV
    coef = summed[:, :qc] * factor[:, None]
    coef_o = summed[:, n : n + qc] * factor[:, None]
    pair = jnp.concatenate([coef, coef_o], axis=1)
    pair_1 = permute(pair, COEF_UP)
    odd_2 = permute(jnp.where(first, coef_o, coef), COEF_UP2)
    coef_2, coef_3 = pair_1[:, :qc], pair_1[:, qc:]

    def correction(doc_coef, window):
        return lax.dot_general(
            doc_coef,
            jnp.concatenate(window, axis=1),
            (((0,), (0,)), ((), ())),
            precision=lax.Precision.HIGHEST,
        )

    even, odd = jnp.where(first, coef, coef_o), jnp.where(first, coef_o, coef)
    even_1, odd_1 = jnp.where(first, coef_2, coef_3), jnp.where(first, coef_3, coef_2)
    window_even = [even, odd_1, even_1, odd_2]
    window_odd = [odd, even, odd_1, even_1]
    window_own = [jnp.where(first, a, b) for a, b in zip(window_even, window_odd)]
    window_o = [jnp.where(first, b, a) for a, b in zip(window_even, window_odd)]
    minus_own = correction(summed[:, qc:n], window_own)
    minus_o = correction(summed[:, n + qc :], window_o)

    none = jnp.zeros((DOC_DEV, qc), jnp.float32)
    flags = jnp.stack([first.astype(jnp.int32), y.astype(jnp.int32)])
    mine, theirs = direct_products(flags, docs, docs_o, (block, up1, cross, even_on, odd_on, crossed))
    direct_own = jnp.concatenate([mine[:, :qc], none, mine[:, qc:], none], axis=1)
    o_0, o_2, o_4 = theirs[:, :qc], theirs[:, qc : 2 * qc], theirs[:, 2 * qc :]
    direct_o = jnp.concatenate(
        [none, jnp.where(first, o_0, o_2), none, jnp.where(first, o_2, o_4)], axis=1
    )
    partial_out = (direct_own - minus_own) + permute(direct_o - minus_o, CORE)
    return reduce_rows(partial_out, x, l).reshape(16, 4, qc)


def solution(mesh):
    in_specs = (
        P("train", "feat"),
        P("train", None),
        P("train", "feat"),
        P("train", None),
        P("train", "feat"),
        P(),
        P(),
    )
    out_specs = P(("train", "feat"), None, None)
    return jax.shard_map(
        per_device, mesh=mesh, in_specs=in_specs, out_specs=out_specs, check_vma=False
    )
```

time: 675 us -> 148 us (0.22)
  waiting for transfers between devices: 613 us -> 50.8 us
  starting transfers between devices: 2.03 us -> 61.3 us
  matrix products: 43.6 us -> 1.26 us
  Pallas kernels: 0 us -> 18.1 us
  between operations: 13.6 us -> 0.43 us
  local copies, waits for them, and re-layouts: 1.84 us -> 13.5 us
    reduce_scatter x4 -> x0, waiting for transfers between devices: 322 us -> none  [per_device(): lax.psum_scatter(term_scores, 'feat', scatter_dimension=0, tiled=True)]
    psum x1 -> x0, waiting for transfers between devices: 157 us -> none  [per_device(): coef = lax.psum(partial_value, 'feat')]
    all_gather x1 -> x0, waiting for transfers between devices: 111 us -> none  [per_device(): all_rows = lax.all_gather(sketch_rows, 'train', axis=0, tiled=True)]
    ppermute x3 -> x23, starting transfers between devices: 1.82 us -> 55.4 us  [permute(): return lax.ppermute(value, BOTH, pairs)]
    dot_general x10 -> x2, matrix products: 43.6 us -> 1.26 us  [correction(): lax.dot_general(doc_coef, jnp.concatenate(window, axis=1), (((0,), (0,)),...]
    pallas_call x0 -> x9, Pallas kernels: none -> 18.1 us  [the longest x1 6.91 us: products(): pl.pallas_call(products_kernel, out_shape=jax.ShapeDtypeStruct((16, 2 * n...]
    ppermute x3 -> x23, waiting for transfers between devices: 21.9 us -> 39 us  [permute(): return lax.ppermute(value, BOTH, pairs)]
    all_to_all x0 -> x1, waiting for transfers between devices: none -> 11.8 us  [per_device(): got = lax.all_to_all(sent, 'feat', 0, 0)]
  transfers between devices with their start and end apart: 9 -> 24, of which waited for: 9 -> 12; matrix products, arithmetic and copies ran while one was open for 5% -> 5% of each run, Pallas kernels for 0% -> 12%
where the time goes in v1:
time: 148 us; the launch traced here: 147 us
  starting transfers between devices  61.3 us (41%)
  waiting for transfers between devices  50.8 us (34%)
  Pallas kernels  18.1 us (12%)
  local copies, waits for them, and re-layouts  13.5 us (9%)
  other arithmetic  1.61 us (1%)
    ppermute x23, starting transfers between devices, permute(): return lax.ppermute(value, BOTH, pairs)  55.4 us
    ppermute x23, waiting for transfers between devices, permute(): return lax.ppermute(value, BOTH, pairs)  39 us
    all_to_all x1, waiting for transfers between devices, per_device(): got = lax.all_to_all(sent, 'feat', 0, 0)  11.8 us
    unnamed x29, local copies, waits for them, and re-layouts  11.5 us
    pallas_call x1, Pallas kernels, products(): pl.pallas_call(products_kernel, out_shape=jax.ShapeDtypeStruct((16, 2 * n...  6.91 us
    all_to_all x1, starting transfers between devices, per_device(): got = lax.all_to_all(sent, 'feat', 0, 0)  5.89 us
    pallas_call x1, Pallas kernels, sum_docs(): pl.pallas_call(docs_kernel, out_shape=jax.ShapeDtypeStruct((DOC_DEV, widt...  5.45 us
    pallas_call x1, Pallas kernels, direct_products(): pl.pallas_call(direct_kernel, out_shape=[jax.ShapeDtypeStruct((DOC_DEV, 2...  5.33 us
  transfers between devices with their start and end apart: 24, of which 12 were waited for; matrix products, arithmetic and copies ran while one was open for 5% of the time, Pallas kernels for 12%

profile of v1, /device:TPU:8, one launch (start us, length us, event | category | flops | bytes accessed | tf_op | source)
XLA Modules:
  0.0 147.0 jit_solution(15756081538411553167)
XLA Ops:
  0.0 2.2 %collective-permute-start.4 = (bf16[64,4096]{1,0:T(8,128)(2,1)}, bf16[64,4096]{1,0:T(8,128)(2,1)}, u32[]{:S(2)}, u32[]{:S(2)}) collective-permute-start(bf16[64,4096]{1,0:T(8,128)(2,1)} %refs_0_.1), channel_id=1, source_target_pairs={{0,96},{1,97},{2,98},{3,99},{4,100},{5,101},{6,102},{7,103},{8,104... | collective-permute-start | bytes 1572872 | tf_op jit(solution)/shard_map/ppermute | solution.py:63
  2.2 1.2 copy-done.9
  3.4 0.7 copy-done.11
  4.1 0.5 pick_rows.1.q_ref.refs_8_
  4.5 0.7 collective-permute-start.1
  5.3 0.1 collective-permute-start.3
  5.4 7.0 %collective-permute-start.2 = (bf16[64,4096]{1,0:T(8,128)(2,1)}, bf16[64,4096]{1,0:T(8,128)(2,1)S(1)}, u32[]{:S(2)}, u32[]{:S(2)}) collective-permute-start(bf16[64,4096]{1,0:T(8,128)(2,1)} %refs_0_.1), channel_id=1, source_target_pairs={{0,128},{1,129},{2,130},{3,131},{4,132},{5,133},{6,134},{7,135},{8... | collective-permute-start | bytes 1572872 | tf_op jit(solution)/shard_map/ppermute | solution.py:63
  12.4 1.6 %collective-permute-done.4.refs_1_ = bf16[64,4096]{1,0:T(8,128)(2,1)} collective-permute-done((bf16[64,4096]{1,0:T(8,128)(2,1)}, bf16[64,4096]{1,0:T(8,128)(2,1)}, u32[]{:S(2)}, u32[]{:S(2)}) %collective-permute-start.4) | collective-permute-done | bytes 524320 | tf_op jit(solution)/shard_map/ppermute | solution.py:63
  14.0 1.0 collective-permute-start.5
  15.0 3.4 %copy-done.3 = bf16[1024,4096]{1,0:T(8,128)(2,1)S(1)} copy-done((bf16[1024,4096]{1,0:T(8,128)(2,1)S(1)}, bf16[1024,4096]{1,0:T(8,128)(2,1)}, u32[]{:S(2)}) %copy-start.3) | copy-done | bytes 8388632
  18.4 5.5 %sum_docs.1.d_ref.refs_9_ = bf16[256,4096]{1,0:T(8,128)(2,1)} custom-call(s32[1,1024]{1,0:T(1,128)S(1)} %copy-done.10, bf16[1024,4096]{1,0:T(8,128)(2,1)S(1)} %copy-done.3), custom_call_target="tpu_custom_call" | custom-call | tf_op jit(solution)/shard_map/sum_docs/pallas_call | solution.py:140
  23.8 0.1 collective-permute-start
  24.0 2.6 %collective-permute-done.2.refs_0_ = bf16[64,4096]{1,0:T(8,128)(2,1)S(1)} collective-permute-done((bf16[64,4096]{1,0:T(8,128)(2,1)}, bf16[64,4096]{1,0:T(8,128)(2,1)S(1)}, u32[]{:S(2)}, u32[]{:S(2)}) %collective-permute-start.2) | collective-permute-done | bytes 524320 | tf_op jit(solution)/shard_map/ppermute | solution.py:63
  26.6 2.1 %collective-permute-done.5.refs_2_ = bf16[64,4096]{1,0:T(8,128)(2,1)} collective-permute-done((bf16[64,4096]{1,0:T(8,128)(2,1)}, bf16[64,4096]{1,0:T(8,128)(2,1)}, u32[]{:S(2)}, u32[]{:S(2)}) %collective-permute-start.5) | collective-permute-done | bytes 524320 | tf_op jit(solution)/shard_map/ppermute | solution.py:63
  28.8 0.0 collective-permute-done.1.up1
  28.8 1.1 broadcast_select_fusion.refs_0_
  29.9 1.8 %collective-permute-start.6 = (bf16[128,4096]{1,0:T(8,128)(2,1)}, bf16[128,4096]{1,0:T(8,128)(2,1)}, u32[]{:S(2)}, u32[]{:S(2)}) collective-permute-start(bf16[128,4096]{1,0:T(8,128)(2,1)} %hold.6), channel_id=1, source_target_pairs={{16,144},{17,145},{18,146},{19,147},{20,148},{21,149},{22,150},{23... | collective-permute-start | bytes 3145736 | tf_op jit(solution)/shard_map/ppermute | solution.py:63
  31.7 8.1 %collective-permute-start.13 = (bf16[128,4096]{1,0:T(8,128)(2,1)S(1)}, bf16[128,4096]{1,0:T(8,128)(2,1)}, u32[]{:S(2)}, u32[]{:S(2)}) collective-permute-start(bf16[128,4096]{1,0:T(8,128)(2,1)S(1)} %pick_rows.1.q_ref.refs_8_), channel_id=1, source_target_pairs={{0,16},{1,17},{2,18},{3,19},{4,20},{5,21},{6,22},{7,23},{8,24},{9,... | collective-permute-start | bytes 3145736 | tf_op jit(solution)/shard_map/ppermute | solution.py:63
  39.7 9.5 %collective-permute-start.7 = (bf16[64,4096]{1,0:T(8,128)(2,1)S(1)}, bf16[64,4096]{1,0:T(8,128)(2,1)S(1)}, u32[]{:S(2)}, u32[]{:S(2)}) collective-permute-start(bf16[64,4096]{1,0:T(8,128)(2,1)S(1)} %copy-done.5), channel_id=1, source_target_pairs={{0,64},{1,65},{2,66},{3,67},{4,68},{5,69},{6,70},{7,71},{8,72},{9,... | collective-permute-start | bytes 1572872 | tf_op jit(solution)/shard_map/ppermute | solution.py:63
  49.2 0.2 collective-permute-start.11
  49.5 12.6 %collective-permute-done.7.refs_1_.refs_6_ = bf16[64,4096]{1,0:T(8,128)(2,1)S(1)} collective-permute-done((bf16[64,4096]{1,0:T(8,128)(2,1)S(1)}, bf16[64,4096]{1,0:T(8,128)(2,1)S(1)}, u32[]{:S(2)}, u32[]{:S(2)}) %collective-permute-start.7) | collective-permute-done | bytes 524320 | tf_op jit(solution)/shard_map/ppermute | solution.py:63
  62.1 0.8 collective-permute-start.12
  62.8 1.0 copy.15.refs_0_
  63.8 1.0 copy.16.refs_0_
  64.8 0.0 collective-permute-done.6.cross
  64.8 1.8 %collective-permute-start.9 = (bf16[128,4096]{1,0:T(8,128)(2,1)}, bf16[128,4096]{1,0:T(8,128)(2,1)}, u32[]{:S(2)}, u32[]{:S(2)}) collective-permute-start(bf16[128,4096]{1,0:T(8,128)(2,1)} %hold.8), channel_id=1, source_target_pairs={{48,80},{49,81},{50,82},{51,83},{52,84},{53,85},{54,86},{55,87},{5... | collective-permute-start | bytes 3145736 | tf_op jit(solution)/shard_map/ppermute | solution.py:63
  66.6 2.3 %copy.17.refs_0_ = bf16[128,4096]{1,0:T(8,128)(2,1)} copy(bf16[128,4096]{1,0:T(8,128)(2,1)} %collective-permute-done.6.cross) | data formatting | bytes 2097152
  69.0 5.1 %collective-permute-start.8 = (bf16[128,4096]{1,0:T(8,128)(2,1)}, bf16[128,4096]{1,0:T(8,128)(2,1)}, u32[]{:S(2)}, u32[]{:S(2)}) collective-permute-start(bf16[128,4096]{1,0:T(8,128)(2,1)} %hold.7), channel_id=1, source_target_pairs={{0,32},{1,33},{2,34},{3,35},{4,36},{5,37},{6,38},{7,39},{8,40},{9,... | collective-permute-start | bytes 3145736 | tf_op jit(solution)/shard_map/ppermute | solution.py:63
  74.1 0.0 collective-permute-done.11.refs_5_
  74.1 1.7 %collective-permute-start.10 = (bf16[128,4096]{1,0:T(8,128)(2,1)}, bf16[128,4096]{1,0:T(8,128)(2,1)}, u32[]{:S(2)}, u32[]{:S(2)}) collective-permute-start(bf16[128,4096]{1,0:T(8,128)(2,1)} %hold.9), channel_id=1, source_target_pairs={{16,48},{17,49},{18,50},{19,51},{20,52},{21,53},{22,54},{23,55},{2... | collective-permute-start | bytes 3145736 | tf_op jit(solution)/shard_map/ppermute | solution.py:63
  75.8 0.1 fusion.1.order_ref
  75.9 0.0 collective-permute-done.do_ref.refs_11_
  75.9 1.0 copy-done.8
  76.9 6.9 %products.1 = bf16[16,32,768]{2,1,0:T(8,128)(2,1)S(1)} custom-call(s32[1]{0:T(128)} %bitcast.2.flag, bf16[256,256]{1,0:T(8,128)(2,1)S(1)} %fusion.1.order_ref, bf16[64,4096]{1,0:T(8,128)(2,1)} %refs_0_.1, bf16[64,4096]{1,0:T(8,128)(2,1)} %collective-permute-done.4.refs_1_, bf16[64,4096]{1,0:T(8,128)(2,1)} %collective-permute-done.5.refs_2_, ...), custom_call_target="tpu_custom_call" | custom-call | tf_op jit(solution)/shard_map/products/pallas_call | solution.py:199
  83.9 0.9 copy-done.6
  84.7 5.9 %all-to-all-start = ((bf16[16,32,768]{2,1,0:T(8,128)(2,1)}), bf16[16,32,768]{2,1,0:T(8,128)(2,1)S(1)}, u32[]{:S(2)}, u32[]{:S(2)}) async-start(bf16[16,32,768]{2,1,0:T(8,128)(2,1)} %copy-done.6), calls=%async_computation | async-start | bytes 1572864 | tf_op jit(solution)/shard_map/all_to_all | solution.py:322
  90.7 0.7 gather_fusion
  91.4 0.7 gather_fusion.1
  92.1 0.1 pad_add_fusion.flags
  92.1 0.0 collective-permute-done.9.odd
  92.2 3.9 %collective-permute-done.8.even = bf16[128,4096]{1,0:T(8,128)(2,1)} collective-permute-done((bf16[128,4096]{1,0:T(8,128)(2,1)}, bf16[128,4096]{1,0:T(8,128)(2,1)}, u32[]{:S(2)}, u32[]{:S(2)}) %collective-permute-start.8) | collective-permute-done | bytes 1048608 | tf_op jit(solution)/shard_map/ppermute | solution.py:63
  96.0 0.0 collective-permute-done.10.on
  96.0 5.3 %direct_products.1 = (f32[256,256]{1,0:T(8,128)S(1)}, f32[256,384]{1,0:T(8,128)S(1)}) custom-call(s32[2]{0:T(128)S(1)} %pad_add_fusion.flags, bf16[256,4096]{1,0:T(8,128)(2,1)} %sum_docs.1.d_ref.refs_9_, bf16[256,4096]{1,0:T(8,128)(2,1)} %collective-permute-done.do_ref.refs_11_, bf16[128,4096]{1,0:T(8,128)(2,1)S(1)} %pick_rows.1.q_ref.refs_8_, ...), custom_call_target="tpu_custom_call" | custom-call | flops 6710886400 | bytes 10485760 | tf_op jit(solution)/shard_map/direct_products/pallas_call | solution.py:237
  101.4 11.8 %all-to-all-done = bf16[16,32,768]{2,1,0:T(8,128)(2,1)S(1)} async-done(((bf16[16,32,768]{2,1,0:T(8,128)(2,1)}), bf16[16,32,768]{2,1,0:T(8,128)(2,1)S(1)}, u32[]{:S(2)}, u32[]{:S(2)}) %all-to-all-start) | async-done | bytes 786464 | tf_op jit(solution)/shard_map/all_to_all | solution.py:322
  113.2 0.1 convert_reduce_fusion
  113.3 0.1 broadcast_select_fusion.8
  113.4 3.8 %collective-permute-start.14 = (f32[32,256]{1,0:T(8,128)S(1)}, f32[32,256]{1,0:T(8,128)S(1)}, u32[]{:S(2)}, u32[]{:S(2)}) collective-permute-start(f32[32,256]{1,0:T(8,128)S(1)} %pad_maximum_fusion), channel_id=1, source_target_pairs={{0,32},{1,33},{2,34},{3,35},{4,36},{5,37},{6,38},{7,39},{8,40},{9,... | collective-permute-start | bytes 98312 | tf_op jit(solution)/shard_map/ppermute | solution.py:63
  117.2 0.1 collective-permute-start.15
  117.3 1.5 %collective-permute-done.14 = f32[32,256]{1,0:T(8,128)S(1)} collective-permute-done((f32[32,256]{1,0:T(8,128)S(1)}, f32[32,256]{1,0:T(8,128)S(1)}, u32[]{:S(2)}, u32[]{:S(2)}) %collective-permute-start.14) | collective-permute-done | bytes 32800 | tf_op jit(solution)/shard_map/ppermute | solution.py:63
  118.8 5.8 %collective-permute-done.15 = f32[32,128]{1,0:T(8,128)S(1)} collective-permute-done((f32[32,128]{1,0:T(8,128)S(1)}, f32[32,128]{1,0:T(8,128)S(1)}, u32[]{:S(2)}, u32[]{:S(2)}) %collective-permute-start.15) | collective-permute-done | bytes 16416 | tf_op jit(solution)/shard_map/ppermute | solution.py:63
  124.7 0.6 convolution_subtract_fusion
  125.3 0.1 collective-permute-start.16
  125.5 1.8 %collective-permute-done.16 = f32[256,512]{1,0:T(8,128)S(1)} collective-permute-done((f32[256,512]{1,0:T(8,128)S(1)}, f32[256,512]{1,0:T(8,128)S(1)}, u32[]{:S(2)}, u32[]{:S(2)}) %collective-permute-start.16) | collective-permute-done | bytes 524320 | tf_op jit(solution)/shard_map/ppermute | solution.py:63
  127.3 0.6 fusion
  128.0 1.6 %collective-permute-start.17 = (f32[64,512]{1,0:T(8,128)S(1)}, f32[64,512]{1,0:T(8,128)S(1)}, u32[]{:S(2)}, u32[]{:S(2)}) collective-permute-start(f32[64,512]{1,0:T(8,128)S(1)} %get-tuple-element.18), channel_id=1, source_target_pairs={{0,8},{1,9},{2,10},{3,11},{4,12},{5,13},{6,14},{7,15},{8,0},{9,1},... | collective-permute-start | bytes 393224 | tf_op jit(solution)/shard_map/ppermute | solution.py:63
  129.6 0.6 collective-permute-start.18
  130.2 2.6 %collective-permute-start.19 = (f32[64,512]{1,0:T(8,128)S(1)}, f32[64,512]{1,0:T(8,128)S(1)}, u32[]{:S(2)}, u32[]{:S(2)}) collective-permute-start(f32[64,512]{1,0:T(8,128)S(1)} %get-tuple-element.19), channel_id=1, source_target_pairs={{0,12},{1,13},{2,14},{3,15},{4,0},{5,1},{6,2},{7,3},{8,4},{9,5},{1... | collective-permute-start | bytes 393224 | tf_op jit(solution)/shard_map/ppermute | solution.py:63
  132.8 3.1 %collective-permute-done.17 = f32[64,512]{1,0:T(8,128)S(1)} collective-permute-done((f32[64,512]{1,0:T(8,128)S(1)}, f32[64,512]{1,0:T(8,128)S(1)}, u32[]{:S(2)}, u32[]{:S(2)}) %collective-permute-start.17) | collective-permute-done | bytes 131104 | tf_op jit(solution)/shard_map/ppermute | solution.py:63
  135.9 2.0 %collective-permute-done.18 = f32[64,512]{1,0:T(8,128)S(1)} collective-permute-done((f32[64,512]{1,0:T(8,128)S(1)}, f32[64,512]{1,0:T(8,128)S(1)}, u32[]{:S(2)}, u32[]{:S(2)}) %collective-permute-start.18) | collective-permute-done | bytes 131104 | tf_op jit(solution)/shard_map/ppermute | solution.py:63
  138.0 2.7 %collective-permute-start.20 = (f32[16,512]{1,0:T(8,128)S(1)}, f32[16,512]{1,0:T(8,128)S(1)}, u32[]{:S(2)}, u32[]{:S(2)}) collective-permute-start(f32[16,512]{1,0:T(8,128)S(1)} %get-tuple-element.25), channel_id=1, source_target_pairs={{0,2},{1,3},{2,0},{3,1},{4,6},{5,7},{6,4},{7,5},{8,10},{9,11},{10,... | collective-permute-start | bytes 98312 | tf_op jit(solution)/shard_map/ppermute | solution.py:63
  140.7 0.0 collective-permute-start.21
  140.7 3.8 %collective-permute-start.22 = (f32[16,512]{1,0:T(8,128)S(1)}, f32[16,512]{1,0:T(8,128)S(1)}, u32[]{:S(2)}, u32[]{:S(2)}) collective-permute-start(f32[16,512]{1,0:T(8,128)S(1)} %get-tuple-element.26), channel_id=1, source_target_pairs={{0,3},{1,0},{2,1},{3,2},{4,7},{5,4},{6,5},{7,6},{8,11},{9,8},{10,9... | collective-permute-start | bytes 98312 | tf_op jit(solution)/shard_map/ppermute | solution.py:63
  144.5 1.9 %collective-permute-done.21 = f32[16,512]{1,0:T(8,128)S(1)} collective-permute-done((f32[16,512]{1,0:T(8,128)S(1)}, f32[16,512]{1,0:T(8,128)S(1)}, u32[]{:S(2)}, u32[]{:S(2)}) %collective-permute-start.21) | collective-permute-done | bytes 32800 | tf_op jit(solution)/shard_map/ppermute | solution.py:63
  146.4 0.6 reshape.152
  (47 shorter events, 0.3 us)
Async XLA Ops:
  0.0 90.7 %copy-start = (f32[1024]{0:T(1024)S(1)}, f32[1024]{0:T(1024)}, u32[]{:S(2)}) copy-start(f32[1024]{0:T(1024)} %param.12) | copy-start | bytes 12292
  0.0 14.0 %collective-permute-start.4 = (bf16[64,4096]{1,0:T(8,128)(2,1)}, bf16[64,4096]{1,0:T(8,128)(2,1)}, u32[]{:S(2)}, u32[]{:S(2)}) collective-permute-start(bf16[64,4096]{1,0:T(8,128)(2,1)} %refs_0_.1), channel_id=1, source_target_pairs={{0,96},{1,97},{2,98},{3,99},{4,100},{5,101},{6,102},{7,103},{8,104... | collective-permute-start | bytes 1572872 | tf_op jit(solution)/shard_map/ppermute | solution.py:63
  2.2 1.2 copy-start.9
  3.4 0.7 copy-start.11
  4.1 10.9 %copy-start.10 = (s32[1,1024]{1,0:T(1,128)S(1)}, s32[1,1024]{1,0:T(1,128)}, u32[]{:S(2)}) copy-start(s32[1,1024]{1,0:T(1,128)} %ids_ref.1) | copy-start | bytes 12292
  4.5 24.2 %collective-permute-start.1 = (bf16[128,4096]{1,0:T(8,128)(2,1)S(1)}, bf16[128,4096]{1,0:T(8,128)(2,1)S(1)}, u32[]{:S(2)}, u32[]{:S(2)}) collective-permute-start(bf16[128,4096]{1,0:T(8,128)(2,1)S(1)} %pick_rows.1.q_ref.refs_8_), channel_id=1, source_target_pairs={{16,48},{17,49},{18,50},{19,51},{20,52},{21,53},{22,54},{23,55},{2... | collective-permute-start | bytes 3145736 | tf_op jit(solution)/shard_map/ppermute | solution.py:63
  5.3 18.7 %collective-permute-start.3 = (bf16[64,4096]{1,0:T(8,128)(2,1)}, bf16[64,4096]{1,0:T(8,128)(2,1)S(1)}, u32[]{:S(2)}, u32[]{:S(2)}) collective-permute-start(bf16[64,4096]{1,0:T(8,128)(2,1)} %refs_0_.1), channel_id=1, source_target_pairs={{0,32},{1,33},{2,34},{3,35},{4,36},{5,37},{6,38},{7,39},{8,40},{9,... | collective-permute-start | bytes 1572872 | tf_op jit(solution)/shard_map/ppermute | solution.py:63
  5.4 21.2 %collective-permute-start.2 = (bf16[64,4096]{1,0:T(8,128)(2,1)}, bf16[64,4096]{1,0:T(8,128)(2,1)S(1)}, u32[]{:S(2)}, u32[]{:S(2)}) collective-permute-start(bf16[64,4096]{1,0:T(8,128)(2,1)} %refs_0_.1), channel_id=1, source_target_pairs={{0,128},{1,129},{2,130},{3,131},{4,132},{5,133},{6,134},{7,135},{8... | collective-permute-start | bytes 1572872 | tf_op jit(solution)/shard_map/ppermute | solution.py:63
  14.0 14.8 %collective-permute-start.5 = (bf16[64,4096]{1,0:T(8,128)(2,1)}, bf16[64,4096]{1,0:T(8,128)(2,1)}, u32[]{:S(2)}, u32[]{:S(2)}) collective-permute-start(bf16[64,4096]{1,0:T(8,128)(2,1)} %collective-permute-done.4.refs_1_), channel_id=1, source_target_pairs={{0,96},{1,97},{2,98},{3,99},{4,100},{5,101},{6,102},{7,103},{8,104... | collective-permute-start | bytes 1572872 | tf_op jit(solution)/shard_map/ppermute | solution.py:63
  15.0 3.4 %copy-start.3 = (bf16[1024,4096]{1,0:T(8,128)(2,1)S(1)}, bf16[1024,4096]{1,0:T(8,128)(2,1)}, u32[]{:S(2)}) copy-start(bf16[1024,4096]{1,0:T(8,128)(2,1)} %rows_ref.2) | copy-start | bytes 25165828
  23.8 52.1 %collective-permute-start = (bf16[256,4096]{1,0:T(8,128)(2,1)}, bf16[256,4096]{1,0:T(8,128)(2,1)}, u32[]{:S(2)}, u32[]{:S(2)}) collective-permute-start(bf16[256,4096]{1,0:T(8,128)(2,1)} %sum_docs.1.d_ref.refs_9_), channel_id=1, source_target_pairs={{0,16},{1,17},{2,18},{3,19},{4,20},{5,21},{6,22},{7,23},{8,24},{9,... | collective-permute-start | bytes 6291464 | tf_op jit(solution)/shard_map/ppermute | solution.py:63
  24.0 4.8 %copy-start.7 = (bf16[64,4096]{1,0:T(8,128)(2,1)}, bf16[64,4096]{1,0:T(8,128)(2,1)S(1)}, u32[]{:S(2)}) copy-start(bf16[64,4096]{1,0:T(8,128)(2,1)S(1)} %collective-permute-done.3.refs_1_.refs_3_) | copy-start | bytes 1572868
  26.6 2.2 %copy-start.4 = (bf16[64,4096]{1,0:T(8,128)(2,1)}, bf16[64,4096]{1,0:T(8,128)(2,1)S(1)}, u32[]{:S(2)}) copy-start(bf16[64,4096]{1,0:T(8,128)(2,1)S(1)} %collective-permute-done.2.refs_0_) | copy-start | bytes 1572868
  29.9 9.9 %copy-start.5 = (bf16[64,4096]{1,0:T(8,128)(2,1)S(1)}, bf16[64,4096]{1,0:T(8,128)(2,1)}, u32[]{:S(2)}) copy-start(bf16[64,4096]{1,0:T(8,128)(2,1)} %hold.5.refs_1_.refs_4_) | copy-start | bytes 1572868
  29.9 34.9 %collective-permute-start.6 = (bf16[128,4096]{1,0:T(8,128)(2,1)}, bf16[128,4096]{1,0:T(8,128)(2,1)}, u32[]{:S(2)}, u32[]{:S(2)}) collective-permute-start(bf16[128,4096]{1,0:T(8,128)(2,1)} %hold.6), channel_id=1, source_target_pairs={{16,144},{17,145},{18,146},{19,147},{20,148},{21,149},{22,150},{23... | collective-permute-start | bytes 3145736 | tf_op jit(solution)/shard_map/ppermute | solution.py:63
  31.7 37.3 %collective-permute-start.13 = (bf16[128,4096]{1,0:T(8,128)(2,1)S(1)}, bf16[128,4096]{1,0:T(8,128)(2,1)}, u32[]{:S(2)}, u32[]{:S(2)}) collective-permute-start(bf16[128,4096]{1,0:T(8,128)(2,1)S(1)} %pick_rows.1.q_ref.refs_8_), channel_id=1, source_target_pairs={{0,16},{1,17},{2,18},{3,19},{4,20},{5,21},{6,22},{7,23},{8,24},{9,... | collective-permute-start | bytes 3145736 | tf_op jit(solution)/shard_map/ppermute | solution.py:63
  39.7 22.3 %collective-permute-start.7 = (bf16[64,4096]{1,0:T(8,128)(2,1)S(1)}, bf16[64,4096]{1,0:T(8,128)(2,1)S(1)}, u32[]{:S(2)}, u32[]{:S(2)}) collective-permute-start(bf16[64,4096]{1,0:T(8,128)(2,1)S(1)} %copy-done.5), channel_id=1, source_target_pairs={{0,64},{1,65},{2,66},{3,67},{4,68},{5,69},{6,70},{7,71},{8,72},{9,... | collective-permute-start | bytes 1572872 | tf_op jit(solution)/shard_map/ppermute | solution.py:63
  49.2 24.9 %collective-permute-start.11 = (bf16[64,4096]{1,0:T(8,128)(2,1)S(1)}, bf16[64,4096]{1,0:T(8,128)(2,1)}, u32[]{:S(2)}, u32[]{:S(2)}) collective-permute-start(bf16[64,4096]{1,0:T(8,128)(2,1)S(1)} %copy-done.5), channel_id=1, source_target_pairs={{0,96},{1,97},{2,98},{3,99},{4,100},{5,101},{6,102},{7,103},{8,104... | collective-permute-start | bytes 1572872 | tf_op jit(solution)/shard_map/ppermute | solution.py:63
  62.0 2.8 %copy-start.1 = (bf16[64,4096]{1,0:T(8,128)(2,1)}, bf16[64,4096]{1,0:T(8,128)(2,1)S(1)}, u32[]{:S(2)}) copy-start(bf16[64,4096]{1,0:T(8,128)(2,1)S(1)} %collective-permute-done.7.refs_1_.refs_6_) | copy-start | bytes 1572868
  62.1 13.8 %collective-permute-start.12 = (bf16[64,4096]{1,0:T(8,128)(2,1)S(1)}, bf16[64,4096]{1,0:T(8,128)(2,1)}, u32[]{:S(2)}, u32[]{:S(2)}) collective-permute-start(bf16[64,4096]{1,0:T(8,128)(2,1)S(1)} %copy-done.5), channel_id=1, source_target_pairs={{0,32},{1,33},{2,34},{3,35},{4,36},{5,37},{6,38},{7,39},{8,40},{9,... | collective-permute-start | bytes 1572872 | tf_op jit(solution)/shard_map/ppermute | solution.py:63
  64.8 11.1 %copy-start.2 = (bf16[64,4096]{1,0:T(8,128)(2,1)S(1)}, bf16[64,4096]{1,0:T(8,128)(2,1)}, u32[]{:S(2)}) copy-start(bf16[64,4096]{1,0:T(8,128)(2,1)} %copy-done.1) | copy-start | bytes 1572868
  64.8 27.3 %collective-permute-start.9 = (bf16[128,4096]{1,0:T(8,128)(2,1)}, bf16[128,4096]{1,0:T(8,128)(2,1)}, u32[]{:S(2)}, u32[]{:S(2)}) collective-permute-start(bf16[128,4096]{1,0:T(8,128)(2,1)} %hold.8), channel_id=1, source_target_pairs={{48,80},{49,81},{50,82},{51,83},{52,84},{53,85},{54,86},{55,87},{5... | collective-permute-start | bytes 3145736 | tf_op jit(solution)/shard_map/ppermute | solution.py:63
  69.0 27.1 %collective-permute-start.8 = (bf16[128,4096]{1,0:T(8,128)(2,1)}, bf16[128,4096]{1,0:T(8,128)(2,1)}, u32[]{:S(2)}, u32[]{:S(2)}) collective-permute-start(bf16[128,4096]{1,0:T(8,128)(2,1)} %hold.7), channel_id=1, source_target_pairs={{0,32},{1,33},{2,34},{3,35},{4,36},{5,37},{6,38},{7,39},{8,40},{9,... | collective-permute-start | bytes 3145736 | tf_op jit(solution)/shard_map/ppermute | solution.py:63
  74.1 21.9 %collective-permute-start.10 = (bf16[128,4096]{1,0:T(8,128)(2,1)}, bf16[128,4096]{1,0:T(8,128)(2,1)}, u32[]{:S(2)}, u32[]{:S(2)}) collective-permute-start(bf16[128,4096]{1,0:T(8,128)(2,1)} %hold.9), channel_id=1, source_target_pairs={{16,48},{17,49},{18,50},{19,51},{20,52},{21,53},{22,54},{23,55},{2... | collective-permute-start | bytes 3145736 | tf_op jit(solution)/shard_map/ppermute | solution.py:63
  75.9 1.0 copy-start.8
  83.9 0.9 copy-start.6
  84.7 6.6 %copy-start.12 = (f32[1024]{0:T(1024)S(1)}, f32[1024]{0:T(1024)}, u32[]{:S(2)}) copy-start(f32[1024]{0:T(1024)} %param.13) | copy-start | bytes 12292
  84.7 28.4 %all-to-all-start = ((bf16[16,32,768]{2,1,0:T(8,128)(2,1)}), bf16[16,32,768]{2,1,0:T(8,128)(2,1)S(1)}, u32[]{:S(2)}, u32[]{:S(2)}) async-start(bf16[16,32,768]{2,1,0:T(8,128)(2,1)} %copy-done.6), calls=%async_computation | async-start | bytes 1572864 | tf_op jit(solution)/shard_map/all_to_all | solution.py:322
  113.4 5.4 %collective-permute-start.14 = (f32[32,256]{1,0:T(8,128)S(1)}, f32[32,256]{1,0:T(8,128)S(1)}, u32[]{:S(2)}, u32[]{:S(2)}) collective-permute-start(f32[32,256]{1,0:T(8,128)S(1)} %pad_maximum_fusion), channel_id=1, source_target_pairs={{0,32},{1,33},{2,34},{3,35},{4,36},{5,37},{6,38},{7,39},{8,40},{9,... | collective-permute-start | bytes 98312 | tf_op jit(solution)/shard_map/ppermute | solution.py:63
  117.2 7.4 %collective-permute-start.15 = (f32[32,128]{1,0:T(8,128)S(1)}, f32[32,128]{1,0:T(8,128)S(1)}, u32[]{:S(2)}, u32[]{:S(2)}) collective-permute-start(f32[32,128]{1,0:T(8,128)S(1)} %get-tuple-element.11), channel_id=1, source_target_pairs={{0,64},{1,65},{2,66},{3,67},{4,68},{5,69},{6,70},{7,71},{8,72},{9,... | collective-permute-start | bytes 49160 | tf_op jit(solution)/shard_map/ppermute | solution.py:63
  125.3 2.0 %collective-permute-start.16 = (f32[256,512]{1,0:T(8,128)S(1)}, f32[256,512]{1,0:T(8,128)S(1)}, u32[]{:S(2)}, u32[]{:S(2)}) collective-permute-start(f32[256,512]{1,0:T(8,128)S(1)} %convolution_subtract_fusion), channel_id=1, source_target_pairs={{0,16},{1,17},{2,18},{3,19},{4,20},{5,21},{6,22},{7,23},{8,24},{9,... | collective-permute-start | bytes 1572872 | tf_op jit(solution)/shard_map/ppermute | solution.py:63
  128.0 7.9 %collective-permute-start.17 = (f32[64,512]{1,0:T(8,128)S(1)}, f32[64,512]{1,0:T(8,128)S(1)}, u32[]{:S(2)}, u32[]{:S(2)}) collective-permute-start(f32[64,512]{1,0:T(8,128)S(1)} %get-tuple-element.18), channel_id=1, source_target_pairs={{0,8},{1,9},{2,10},{3,11},{4,12},{5,13},{6,14},{7,15},{8,0},{9,1},... | collective-permute-start | bytes 393224 | tf_op jit(solution)/shard_map/ppermute | solution.py:63
  129.6 8.4 %collective-permute-start.18 = (f32[64,512]{1,0:T(8,128)S(1)}, f32[64,512]{1,0:T(8,128)S(1)}, u32[]{:S(2)}, u32[]{:S(2)}) collective-permute-start(f32[64,512]{1,0:T(8,128)S(1)} %get-tuple-element.20), channel_id=1, source_target_pairs={{0,4},{1,5},{2,6},{3,7},{4,8},{5,9},{6,10},{7,11},{8,12},{9,13},{1... | collective-permute-start | bytes 393224 | tf_op jit(solution)/shard_map/ppermute | solution.py:63
  130.2 7.8 %collective-permute-start.19 = (f32[64,512]{1,0:T(8,128)S(1)}, f32[64,512]{1,0:T(8,128)S(1)}, u32[]{:S(2)}, u32[]{:S(2)}) collective-permute-start(f32[64,512]{1,0:T(8,128)S(1)} %get-tuple-element.19), channel_id=1, source_target_pairs={{0,12},{1,13},{2,14},{3,15},{4,0},{5,1},{6,2},{7,3},{8,4},{9,5},{1... | collective-permute-start | bytes 393224 | tf_op jit(solution)/shard_map/ppermute | solution.py:63
  138.0 6.5 %collective-permute-start.20 = (f32[16,512]{1,0:T(8,128)S(1)}, f32[16,512]{1,0:T(8,128)S(1)}, u32[]{:S(2)}, u32[]{:S(2)}) collective-permute-start(f32[16,512]{1,0:T(8,128)S(1)} %get-tuple-element.25), channel_id=1, source_target_pairs={{0,2},{1,3},{2,0},{3,1},{4,6},{5,7},{6,4},{7,5},{8,10},{9,11},{10,... | collective-permute-start | bytes 98312 | tf_op jit(solution)/shard_map/ppermute | solution.py:63
  140.7 5.7 %collective-permute-start.21 = (f32[16,512]{1,0:T(8,128)S(1)}, f32[16,512]{1,0:T(8,128)S(1)}, u32[]{:S(2)}, u32[]{:S(2)}) collective-permute-start(f32[16,512]{1,0:T(8,128)S(1)} %get-tuple-element.27), channel_id=1, source_target_pairs={{0,1},{1,2},{2,3},{3,0},{4,5},{5,6},{6,7},{7,4},{8,9},{9,10},{10,1... | collective-permute-start | bytes 98312 | tf_op jit(solution)/shard_map/ppermute | solution.py:63
  140.7 5.7 %collective-permute-start.22 = (f32[16,512]{1,0:T(8,128)S(1)}, f32[16,512]{1,0:T(8,128)S(1)}, u32[]{:S(2)}, u32[]{:S(2)}) collective-permute-start(f32[16,512]{1,0:T(8,128)S(1)} %get-tuple-element.26), channel_id=1, source_target_pairs={{0,3},{1,0},{2,1},{3,2},{4,7},{5,4},{6,5},{7,6},{8,11},{9,8},{10,9... | collective-permute-start | bytes 98312 | tf_op jit(solution)/shard_map/ppermute | solution.py:63

commit v2 on v1

--- a/solution.py
+++ b/solution.py
@@ -316,7 +316,7 @@
     cross = permute(hold(jnp.where(bottom, up1, block), far_own), CROSS)
     even_on = permute(hold(block, far_opposite), EVEN_UP)
     odd_on = permute(hold(up1, far_opposite), ODD_AGAIN)
-    crossed = permute(hold(cross, far_opposite), CROSSED_ON)
+    crossed = permute(cross, CROSSED_ON)
 
     sent = products(z.reshape(1), order, near, far, others)
     got = lax.all_to_all(sent, "feat", 0, 0)

time: 148 us -> 143 us (0.966)
  starting transfers between devices: 61.3 us -> 53.2 us
  waiting for transfers between devices: 50.8 us -> 54.6 us
    ppermute x23, waiting for transfers between devices: 39 us -> 48 us  [permute(): return lax.ppermute(value, BOTH, pairs)]
    ppermute x23, starting transfers between devices: 55.4 us -> 47.2 us  [permute(): return lax.ppermute(value, BOTH, pairs)]
    all_to_all x1, waiting for transfers between devices: 11.8 us -> 6.59 us  [per_device(): got = lax.all_to_all(sent, 'feat', 0, 0)]
    unnamed x29 -> x20, local copies, waits for them, and re-layouts: 11.5 us -> 10.2 us
  transfers between devices with their start and end apart: 24 -> 24, of which waited for: 12 -> 12; matrix products, arithmetic and copies ran while one was open for 5% -> 4% of each run, Pallas kernels for 12% -> 12%
where the time goes in v2:
time: 143 us; the launch traced here: 142 us
  waiting for transfers between devices  54.6 us (38%)
  starting transfers between devices  53.2 us (37%)
  Pallas kernels  17.4 us (12%)
  local copies, waits for them, and re-layouts  12.2 us (9%)
  other arithmetic  2.93 us (2%)
    ppermute x23, waiting for transfers between devices, permute(): return lax.ppermute(value, BOTH, pairs)  48 us
    ppermute x23, starting transfers between devices, permute(): return lax.ppermute(value, BOTH, pairs)  47.2 us
    unnamed x20, local copies, waits for them, and re-layouts  10.2 us
    pallas_call x1, Pallas kernels, products(): pl.pallas_call(products_kernel, out_shape=jax.ShapeDtypeStruct((16, 2 * n...  6.83 us
    all_to_all x1, waiting for transfers between devices, per_device(): got = lax.all_to_all(sent, 'feat', 0, 0)  6.59 us
    all_to_all x1, starting transfers between devices, per_device(): got = lax.all_to_all(sent, 'feat', 0, 0)  6.02 us
    pallas_call x1, Pallas kernels, sum_docs(): pl.pallas_call(docs_kernel, out_shape=jax.ShapeDtypeStruct((DOC_DEV, widt...  5.07 us
    pallas_call x1, Pallas kernels, direct_products(): pl.pallas_call(direct_kernel, out_shape=[jax.ShapeDtypeStruct((DOC_DEV, 2...  4.99 us
  transfers between devices with their start and end apart: 24, of which 12 were waited for; matrix products, arithmetic and copies ran while one was open for 4% of the time, Pallas kernels for 12%

profile of v2, /device:TPU:8, one launch (start us, length us, event | category | flops | bytes accessed | tf_op | source)
XLA Modules:
  0.0 141.9 jit_solution(11176465530227749465)
XLA Ops:
  0.0 1.2 copy-done.3
  1.2 0.7 copy-done.7
  1.9 0.5 pick_rows.1.q_ref.refs_8_
  2.4 1.6 %collective-permute-start.1 = (bf16[128,4096]{1,0:T(8,128)(2,1)S(1)}, bf16[128,4096]{1,0:T(8,128)(2,1)}, u32[]{:S(2)}, u32[]{:S(2)}) collective-permute-start(bf16[128,4096]{1,0:T(8,128)(2,1)S(1)} %pick_rows.1.q_ref.refs_8_), channel_id=1, source_target_pairs={{16,48},{17,49},{18,50},{19,51},{20,52},{21,53},{22,54},{23,55},{2... | collective-permute-start | bytes 3145736 | tf_op jit(solution)/shard_map/ppermute | solution.py:63
  4.0 2.2 %collective-permute-start.4 = (bf16[64,4096]{1,0:T(8,128)(2,1)}, bf16[64,4096]{1,0:T(8,128)(2,1)}, u32[]{:S(2)}, u32[]{:S(2)}) collective-permute-start(bf16[64,4096]{1,0:T(8,128)(2,1)} %refs_0_.1), channel_id=1, source_target_pairs={{0,96},{1,97},{2,98},{3,99},{4,100},{5,101},{6,102},{7,103},{8,104... | collective-permute-start | bytes 1572872 | tf_op jit(solution)/shard_map/ppermute | solution.py:63
  6.2 0.0 collective-permute-start.3
  6.2 7.0 %collective-permute-start.2 = (bf16[64,4096]{1,0:T(8,128)(2,1)}, bf16[64,4096]{1,0:T(8,128)(2,1)}, u32[]{:S(2)}, u32[]{:S(2)}) collective-permute-start(bf16[64,4096]{1,0:T(8,128)(2,1)} %refs_0_.1), channel_id=1, source_target_pairs={{0,128},{1,129},{2,130},{3,131},{4,132},{5,133},{6,134},{7,135},{8... | collective-permute-start | bytes 1572872 | tf_op jit(solution)/shard_map/ppermute | solution.py:63
  13.2 0.6 collective-permute-start.13
  13.9 3.4 %copy-done.1 = bf16[1024,4096]{1,0:T(8,128)(2,1)S(1)} copy-done((bf16[1024,4096]{1,0:T(8,128)(2,1)S(1)}, bf16[1024,4096]{1,0:T(8,128)(2,1)}, u32[]{:S(2)}) %copy-start.1) | copy-done | bytes 8388632
  17.3 5.1 %sum_docs.1.d_ref.refs_9_ = bf16[256,4096]{1,0:T(8,128)(2,1)S(1)} custom-call(s32[1,1024]{1,0:T(1,128)S(1)} %copy-done.6, bf16[1024,4096]{1,0:T(8,128)(2,1)S(1)} %copy-done.1), custom_call_target="tpu_custom_call" | custom-call | tf_op jit(solution)/shard_map/sum_docs/pallas_call | solution.py:140
  22.3 0.0 collective-permute-done.4.refs_1_
  22.3 0.1 collective-permute-start
  22.4 0.0 collective-permute-done.1.up1
  22.5 1.3 collective-permute-start.5
  23.7 1.3 broadcast_select_fusion.refs_0_
  25.0 0.0 collective-permute-done.3.refs_1_.refs_3_
  25.0 11.6 %collective-permute-done.2.refs_0_ = bf16[64,4096]{1,0:T(8,128)(2,1)} collective-permute-done((bf16[64,4096]{1,0:T(8,128)(2,1)}, bf16[64,4096]{1,0:T(8,128)(2,1)}, u32[]{:S(2)}, u32[]{:S(2)}) %collective-permute-start.2) | collective-permute-done | bytes 524320 | tf_op jit(solution)/shard_map/ppermute | solution.py:63
  36.6 0.8 collective-permute-done.5.refs_2_
  37.4 1.7 %collective-permute-start.6 = (bf16[128,4096]{1,0:T(8,128)(2,1)}, bf16[128,4096]{1,0:T(8,128)(2,1)}, u32[]{:S(2)}, u32[]{:S(2)}) collective-permute-start(bf16[128,4096]{1,0:T(8,128)(2,1)} %hold.5), channel_id=1, source_target_pairs={{16,144},{17,145},{18,146},{19,147},{20,148},{21,149},{22,150},{23... | collective-permute-start | bytes 3145736 | tf_op jit(solution)/shard_map/ppermute | solution.py:63
  39.1 8.0 %collective-permute-start.7 = (bf16[64,4096]{1,0:T(8,128)(2,1)}, bf16[64,4096]{1,0:T(8,128)(2,1)}, u32[]{:S(2)}, u32[]{:S(2)}) collective-permute-start(bf16[64,4096]{1,0:T(8,128)(2,1)} %hold.4.refs_1_.refs_4_), channel_id=1, source_target_pairs={{0,64},{1,65},{2,66},{3,67},{4,68},{5,69},{6,70},{7,71},{8,72},{9,... | collective-permute-start | bytes 1572872 | tf_op jit(solution)/shard_map/ppermute | solution.py:63
  47.0 13.2 %collective-permute-done.7.refs_1_.refs_6_ = bf16[64,4096]{1,0:T(8,128)(2,1)} collective-permute-done((bf16[64,4096]{1,0:T(8,128)(2,1)}, bf16[64,4096]{1,0:T(8,128)(2,1)}, u32[]{:S(2)}, u32[]{:S(2)}) %collective-permute-start.7) | collective-permute-done | bytes 524320 | tf_op jit(solution)/shard_map/ppermute | solution.py:63
  60.2 1.0 copy.14.refs_0_
  61.2 2.3 %copy.15.refs_0_ = bf16[128,4096]{1,0:T(8,128)(2,1)} copy(bf16[128,4096]{1,0:T(8,128)(2,1)} %collective-permute-done.1.up1) | data formatting | bytes 2097152
  63.5 0.0 collective-permute-done.13.refs_10_
  63.5 1.6 %collective-permute-start.9 = (bf16[128,4096]{1,0:T(8,128)(2,1)}, bf16[128,4096]{1,0:T(8,128)(2,1)}, u32[]{:S(2)}, u32[]{:S(2)}) collective-permute-start(bf16[128,4096]{1,0:T(8,128)(2,1)} %hold.7), channel_id=1, source_target_pairs={{48,80},{49,81},{50,82},{51,83},{52,84},{53,85},{54,86},{55,87},{5... | collective-permute-start | bytes 3145736 | tf_op jit(solution)/shard_map/ppermute | solution.py:63
  65.2 1.0 collective-permute-done.11.refs_5_
  66.2 5.0 %collective-permute-start.8 = (bf16[128,4096]{1,0:T(8,128)(2,1)}, bf16[128,4096]{1,0:T(8,128)(2,1)}, u32[]{:S(2)}, u32[]{:S(2)}) collective-permute-start(bf16[128,4096]{1,0:T(8,128)(2,1)} %hold.6), channel_id=1, source_target_pairs={{0,32},{1,33},{2,34},{3,35},{4,36},{5,37},{6,38},{7,39},{8,40},{9,... | collective-permute-start | bytes 3145736 | tf_op jit(solution)/shard_map/ppermute | solution.py:63
  71.1 0.0 collective-permute-done.6.cross
  71.1 1.7 %collective-permute-start.10 = (bf16[128,4096]{1,0:T(8,128)(2,1)}, bf16[128,4096]{1,0:T(8,128)(2,1)}, u32[]{:S(2)}, u32[]{:S(2)}) collective-permute-start(bf16[128,4096]{1,0:T(8,128)(2,1)} %collective-permute-done.6.cross), channel_id=1, source_target_pairs={{16,48},{17,49},{18,50},{19,51},{20,52},{21,53},{22,54},{23,55},{2... | collective-permute-start | bytes 3145736 | tf_op jit(solution)/shard_map/ppermute | solution.py:63
  72.9 0.1 fusion.1.order_ref
  73.0 0.0 collective-permute-done.do_ref.refs_11_
  73.0 6.8 %products.1 = bf16[16,32,768]{2,1,0:T(8,128)(2,1)S(1)} custom-call(s32[1]{0:T(128)} %bitcast.2.flag, bf16[256,256]{1,0:T(8,128)(2,1)S(1)} %fusion.1.order_ref, bf16[64,4096]{1,0:T(8,128)(2,1)} %refs_0_.1, bf16[64,4096]{1,0:T(8,128)(2,1)} %collective-permute-done.4.refs_1_, bf16[64,4096]{1,0:T(8,128)(2,1)} %collective-permute-done.5.refs_2_, ...), custom_call_target="tpu_custom_call" | custom-call | tf_op jit(solution)/shard_map/products/pallas_call | solution.py:199
  79.9 0.9 copy-done.2
  80.7 6.0 %all-to-all-start = ((bf16[16,32,768]{2,1,0:T(8,128)(2,1)}), bf16[16,32,768]{2,1,0:T(8,128)(2,1)}, u32[]{:S(2)}, u32[]{:S(2)}) async-start(bf16[16,32,768]{2,1,0:T(8,128)(2,1)} %copy-done.2), calls=%async_computation | async-start | bytes 1572864 | tf_op jit(solution)/shard_map/all_to_all | solution.py:322
  86.8 0.7 gather_fusion
  87.5 0.7 gather_fusion.1
  88.2 0.1 pad_add_fusion.flags
  88.3 0.0 collective-permute-done.9.odd
  88.3 6.0 %collective-permute-done.8.even = bf16[128,4096]{1,0:T(8,128)(2,1)} collective-permute-done((bf16[128,4096]{1,0:T(8,128)(2,1)}, bf16[128,4096]{1,0:T(8,128)(2,1)}, u32[]{:S(2)}, u32[]{:S(2)}) %collective-permute-start.8) | collective-permute-done | bytes 1048608 | tf_op jit(solution)/shard_map/ppermute | solution.py:63
  94.3 5.0 %direct_products.1 = (f32[256,256]{1,0:T(8,128)S(1)}, f32[256,384]{1,0:T(8,128)S(1)}) custom-call(s32[2]{0:T(128)S(1)} %pad_add_fusion.flags, bf16[256,4096]{1,0:T(8,128)(2,1)S(1)} %sum_docs.1.d_ref.refs_9_, bf16[256,4096]{1,0:T(8,128)(2,1)} %collective-permute-done.do_ref.refs_11_, bf16[128,4096]{1,0:T(8,128)(2,1)S(1)} %pick_rows.1.q_ref.refs_8_, ...), custom_call_target="tpu_custom_call" | custom-call | flops 6710886400 | bytes 10485760 | tf_op jit(solution)/shard_map/direct_products/pallas_call | solution.py:237
  99.3 0.7 copy-done.4
  100.0 6.6 %all-to-all-done = bf16[16,32,768]{2,1,0:T(8,128)(2,1)} async-done(((bf16[16,32,768]{2,1,0:T(8,128)(2,1)}), bf16[16,32,768]{2,1,0:T(8,128)(2,1)}, u32[]{:S(2)}, u32[]{:S(2)}) %all-to-all-start) | async-done | bytes 786464 | tf_op jit(solution)/shard_map/all_to_all | solution.py:322
  106.6 1.3 convert_reduce_fusion
  107.9 0.1 broadcast_select_fusion.8
  108.0 3.9 %collective-permute-start.14 = (f32[32,256]{1,0:T(8,128)S(1)}, f32[32,256]{1,0:T(8,128)S(1)}, u32[]{:S(2)}, u32[]{:S(2)}) collective-permute-start(f32[32,256]{1,0:T(8,128)S(1)} %pad_maximum_fusion), channel_id=1, source_target_pairs={{0,32},{1,33},{2,34},{3,35},{4,36},{5,37},{6,38},{7,39},{8,40},{9,... | collective-permute-start | bytes 98312 | tf_op jit(solution)/shard_map/ppermute | solution.py:63
  111.9 0.1 collective-permute-start.15
  112.0 1.5 %collective-permute-done.14 = f32[32,256]{1,0:T(8,128)S(1)} collective-permute-done((f32[32,256]{1,0:T(8,128)S(1)}, f32[32,256]{1,0:T(8,128)S(1)}, u32[]{:S(2)}, u32[]{:S(2)}) %collective-permute-start.14) | collective-permute-done | bytes 32800 | tf_op jit(solution)/shard_map/ppermute | solution.py:63
  113.5 5.9 %collective-permute-done.15 = f32[32,128]{1,0:T(8,128)S(1)} collective-permute-done((f32[32,128]{1,0:T(8,128)S(1)}, f32[32,128]{1,0:T(8,128)S(1)}, u32[]{:S(2)}, u32[]{:S(2)}) %collective-permute-start.15) | collective-permute-done | bytes 16416 | tf_op jit(solution)/shard_map/ppermute | solution.py:63
  119.5 0.6 convolution_subtract_fusion
  120.1 0.2 collective-permute-start.16
  120.3 1.8 %collective-permute-done.16 = f32[256,512]{1,0:T(8,128)S(1)} collective-permute-done((f32[256,512]{1,0:T(8,128)S(1)}, f32[256,512]{1,0:T(8,128)S(1)}, u32[]{:S(2)}, u32[]{:S(2)}) %collective-permute-start.16) | collective-permute-done | bytes 524320 | tf_op jit(solution)/shard_map/ppermute | solution.py:63
  122.1 0.6 fusion
  122.8 2.4 %collective-permute-start.17 = (f32[64,512]{1,0:T(8,128)S(1)}, f32[64,512]{1,0:T(8,128)S(1)}, u32[]{:S(2)}, u32[]{:S(2)}) collective-permute-start(f32[64,512]{1,0:T(8,128)S(1)} %get-tuple-element.18), channel_id=1, source_target_pairs={{0,8},{1,9},{2,10},{3,11},{4,12},{5,13},{6,14},{7,15},{8,0},{9,1},... | collective-permute-start | bytes 393224 | tf_op jit(solution)/shard_map/ppermute | solution.py:63
  125.1 0.6 collective-permute-start.18
  125.7 2.6 %collective-permute-start.19 = (f32[64,512]{1,0:T(8,128)S(1)}, f32[64,512]{1,0:T(8,128)S(1)}, u32[]{:S(2)}, u32[]{:S(2)}) collective-permute-start(f32[64,512]{1,0:T(8,128)S(1)} %get-tuple-element.19), channel_id=1, source_target_pairs={{0,12},{1,13},{2,14},{3,15},{4,0},{5,1},{6,2},{7,3},{8,4},{9,5},{1... | collective-permute-start | bytes 393224 | tf_op jit(solution)/shard_map/ppermute | solution.py:63
  128.4 2.3 %collective-permute-done.17 = f32[64,512]{1,0:T(8,128)S(1)} collective-permute-done((f32[64,512]{1,0:T(8,128)S(1)}, f32[64,512]{1,0:T(8,128)S(1)}, u32[]{:S(2)}, u32[]{:S(2)}) %collective-permute-start.17) | collective-permute-done | bytes 131104 | tf_op jit(solution)/shard_map/ppermute | solution.py:63
  130.7 2.0 %collective-permute-done.18 = f32[64,512]{1,0:T(8,128)S(1)} collective-permute-done((f32[64,512]{1,0:T(8,128)S(1)}, f32[64,512]{1,0:T(8,128)S(1)}, u32[]{:S(2)}, u32[]{:S(2)}) %collective-permute-start.18) | collective-permute-done | bytes 131104 | tf_op jit(solution)/shard_map/ppermute | solution.py:63
  132.7 0.0 collective-permute-done.19
  132.8 2.7 %collective-permute-start.20 = (f32[16,512]{1,0:T(8,128)S(1)}, f32[16,512]{1,0:T(8,128)S(1)}, u32[]{:S(2)}, u32[]{:S(2)}) collective-permute-start(f32[16,512]{1,0:T(8,128)S(1)} %get-tuple-element.25), channel_id=1, source_target_pairs={{0,2},{1,3},{2,0},{3,1},{4,6},{5,7},{6,4},{7,5},{8,10},{9,11},{10,... | collective-permute-start | bytes 98312 | tf_op jit(solution)/shard_map/ppermute | solution.py:63
  135.6 0.2 collective-permute-start.21
  135.8 3.6 %collective-permute-start.22 = (f32[16,512]{1,0:T(8,128)S(1)}, f32[16,512]{1,0:T(8,128)S(1)}, u32[]{:S(2)}, u32[]{:S(2)}) collective-permute-start(f32[16,512]{1,0:T(8,128)S(1)} %get-tuple-element.26), channel_id=1, source_target_pairs={{0,3},{1,0},{2,1},{3,2},{4,7},{5,4},{6,5},{7,6},{8,11},{9,8},{10,9... | collective-permute-start | bytes 98312 | tf_op jit(solution)/shard_map/ppermute | solution.py:63
  139.4 0.0 collective-permute-done.20
  139.4 1.9 %collective-permute-done.21 = f32[16,512]{1,0:T(8,128)S(1)} collective-permute-done((f32[16,512]{1,0:T(8,128)S(1)}, f32[16,512]{1,0:T(8,128)S(1)}, u32[]{:S(2)}, u32[]{:S(2)}) %collective-permute-start.21) | collective-permute-done | bytes 32800 | tf_op jit(solution)/shard_map/ppermute | solution.py:63
  141.3 0.6 reshape.152
  (37 shorter events, 0.3 us)
Async XLA Ops:
  0.0 86.8 %copy-start = (f32[1024]{0:T(1024)S(1)}, f32[1024]{0:T(1024)}, u32[]{:S(2)}) copy-start(f32[1024]{0:T(1024)} %param.12) | copy-start | bytes 12292
  0.0 1.2 copy-start.3
  1.2 0.7 copy-start.7
  1.9 12.0 %copy-start.6 = (s32[1,1024]{1,0:T(1,128)S(1)}, s32[1,1024]{1,0:T(1,128)}, u32[]{:S(2)}) copy-start(s32[1,1024]{1,0:T(1,128)} %ids_ref.1) | copy-start | bytes 12292
  2.4 20.1 %collective-permute-start.1 = (bf16[128,4096]{1,0:T(8,128)(2,1)S(1)}, bf16[128,4096]{1,0:T(8,128)(2,1)}, u32[]{:S(2)}, u32[]{:S(2)}) collective-permute-start(bf16[128,4096]{1,0:T(8,128)(2,1)S(1)} %pick_rows.1.q_ref.refs_8_), channel_id=1, source_target_pairs={{16,48},{17,49},{18,50},{19,51},{20,52},{21,53},{22,54},{23,55},{2... | collective-permute-start | bytes 3145736 | tf_op jit(solution)/shard_map/ppermute | solution.py:63
  4.0 18.3 %collective-permute-start.4 = (bf16[64,4096]{1,0:T(8,128)(2,1)}, bf16[64,4096]{1,0:T(8,128)(2,1)}, u32[]{:S(2)}, u32[]{:S(2)}) collective-permute-start(bf16[64,4096]{1,0:T(8,128)(2,1)} %refs_0_.1), channel_id=1, source_target_pairs={{0,96},{1,97},{2,98},{3,99},{4,100},{5,101},{6,102},{7,103},{8,104... | collective-permute-start | bytes 1572872 | tf_op jit(solution)/shard_map/ppermute | solution.py:63
  6.2 18.8 %collective-permute-start.3 = (bf16[64,4096]{1,0:T(8,128)(2,1)}, bf16[64,4096]{1,0:T(8,128)(2,1)}, u32[]{:S(2)}, u32[]{:S(2)}) collective-permute-start(bf16[64,4096]{1,0:T(8,128)(2,1)} %refs_0_.1), channel_id=1, source_target_pairs={{0,32},{1,33},{2,34},{3,35},{4,36},{5,37},{6,38},{7,39},{8,40},{9,... | collective-permute-start | bytes 1572872 | tf_op jit(solution)/shard_map/ppermute | solution.py:63
  6.2 30.4 %collective-permute-start.2 = (bf16[64,4096]{1,0:T(8,128)(2,1)}, bf16[64,4096]{1,0:T(8,128)(2,1)}, u32[]{:S(2)}, u32[]{:S(2)}) collective-permute-start(bf16[64,4096]{1,0:T(8,128)(2,1)} %refs_0_.1), channel_id=1, source_target_pairs={{0,128},{1,129},{2,130},{3,131},{4,132},{5,133},{6,134},{7,135},{8... | collective-permute-start | bytes 1572872 | tf_op jit(solution)/shard_map/ppermute | solution.py:63
  13.2 50.3 %collective-permute-start.13 = (bf16[128,4096]{1,0:T(8,128)(2,1)S(1)}, bf16[128,4096]{1,0:T(8,128)(2,1)}, u32[]{:S(2)}, u32[]{:S(2)}) collective-permute-start(bf16[128,4096]{1,0:T(8,128)(2,1)S(1)} %pick_rows.1.q_ref.refs_8_), channel_id=1, source_target_pairs={{0,16},{1,17},{2,18},{3,19},{4,20},{5,21},{6,22},{7,23},{8,24},{9,... | collective-permute-start | bytes 3145736 | tf_op jit(solution)/shard_map/ppermute | solution.py:63
  13.9 3.4 %copy-start.1 = (bf16[1024,4096]{1,0:T(8,128)(2,1)S(1)}, bf16[1024,4096]{1,0:T(8,128)(2,1)}, u32[]{:S(2)}) copy-start(bf16[1024,4096]{1,0:T(8,128)(2,1)} %rows_ref.2) | copy-start | bytes 25165828
  22.3 50.7 %collective-permute-start = (bf16[256,4096]{1,0:T(8,128)(2,1)S(1)}, bf16[256,4096]{1,0:T(8,128)(2,1)}, u32[]{:S(2)}, u32[]{:S(2)}) collective-permute-start(bf16[256,4096]{1,0:T(8,128)(2,1)S(1)} %sum_docs.1.d_ref.refs_9_), channel_id=1, source_target_pairs={{0,16},{1,17},{2,18},{3,19},{4,20},{5,21},{6,22},{7,23},{8,24},{9,... | collective-permute-start | bytes 6291464 | tf_op jit(solution)/shard_map/ppermute | solution.py:63
  22.5 14.9 %collective-permute-start.5 = (bf16[64,4096]{1,0:T(8,128)(2,1)}, bf16[64,4096]{1,0:T(8,128)(2,1)}, u32[]{:S(2)}, u32[]{:S(2)}) collective-permute-start(bf16[64,4096]{1,0:T(8,128)(2,1)} %collective-permute-done.4.refs_1_), channel_id=1, source_target_pairs={{0,96},{1,97},{2,98},{3,99},{4,100},{5,101},{6,102},{7,103},{8,104... | collective-permute-start | bytes 1572872 | tf_op jit(solution)/shard_map/ppermute | solution.py:63
  37.4 33.8 %collective-permute-start.6 = (bf16[128,4096]{1,0:T(8,128)(2,1)}, bf16[128,4096]{1,0:T(8,128)(2,1)}, u32[]{:S(2)}, u32[]{:S(2)}) collective-permute-start(bf16[128,4096]{1,0:T(8,128)(2,1)} %hold.5), channel_id=1, source_target_pairs={{16,144},{17,145},{18,146},{19,147},{20,148},{21,149},{22,150},{23... | collective-permute-start | bytes 3145736 | tf_op jit(solution)/shard_map/ppermute | solution.py:63
  39.1 21.1 %collective-permute-start.7 = (bf16[64,4096]{1,0:T(8,128)(2,1)}, bf16[64,4096]{1,0:T(8,128)(2,1)}, u32[]{:S(2)}, u32[]{:S(2)}) collective-permute-start(bf16[64,4096]{1,0:T(8,128)(2,1)} %hold.4.refs_1_.refs_4_), channel_id=1, source_target_pairs={{0,64},{1,65},{2,66},{3,67},{4,68},{5,69},{6,70},{7,71},{8,72},{9,... | collective-permute-start | bytes 1572872 | tf_op jit(solution)/shard_map/ppermute | solution.py:63
  47.0 19.1 %collective-permute-start.11 = (bf16[64,4096]{1,0:T(8,128)(2,1)}, bf16[64,4096]{1,0:T(8,128)(2,1)}, u32[]{:S(2)}, u32[]{:S(2)}) collective-permute-start(bf16[64,4096]{1,0:T(8,128)(2,1)} %hold.4.refs_1_.refs_4_), channel_id=1, source_target_pairs={{0,96},{1,97},{2,98},{3,99},{4,100},{5,101},{6,102},{7,103},{8,104... | collective-permute-start | bytes 1572872 | tf_op jit(solution)/shard_map/ppermute | solution.py:63
  60.2 12.8 %collective-permute-start.12 = (bf16[64,4096]{1,0:T(8,128)(2,1)}, bf16[64,4096]{1,0:T(8,128)(2,1)}, u32[]{:S(2)}, u32[]{:S(2)}) collective-permute-start(bf16[64,4096]{1,0:T(8,128)(2,1)} %hold.4.refs_1_.refs_4_), channel_id=1, source_target_pairs={{0,32},{1,33},{2,34},{3,35},{4,36},{5,37},{6,38},{7,39},{8,40},{9,... | collective-permute-start | bytes 1572872 | tf_op jit(solution)/shard_map/ppermute | solution.py:63
  63.5 24.8 %collective-permute-start.9 = (bf16[128,4096]{1,0:T(8,128)(2,1)}, bf16[128,4096]{1,0:T(8,128)(2,1)}, u32[]{:S(2)}, u32[]{:S(2)}) collective-permute-start(bf16[128,4096]{1,0:T(8,128)(2,1)} %hold.7), channel_id=1, source_target_pairs={{48,80},{49,81},{50,82},{51,83},{52,84},{53,85},{54,86},{55,87},{5... | collective-permute-start | bytes 3145736 | tf_op jit(solution)/shard_map/ppermute | solution.py:63
  66.2 28.1 %collective-permute-start.8 = (bf16[128,4096]{1,0:T(8,128)(2,1)}, bf16[128,4096]{1,0:T(8,128)(2,1)}, u32[]{:S(2)}, u32[]{:S(2)}) collective-permute-start(bf16[128,4096]{1,0:T(8,128)(2,1)} %hold.6), channel_id=1, source_target_pairs={{0,32},{1,33},{2,34},{3,35},{4,36},{5,37},{6,38},{7,39},{8,40},{9,... | collective-permute-start | bytes 3145736 | tf_op jit(solution)/shard_map/ppermute | solution.py:63
  71.1 23.1 %collective-permute-start.10 = (bf16[128,4096]{1,0:T(8,128)(2,1)}, bf16[128,4096]{1,0:T(8,128)(2,1)}, u32[]{:S(2)}, u32[]{:S(2)}) collective-permute-start(bf16[128,4096]{1,0:T(8,128)(2,1)} %collective-permute-done.6.cross), channel_id=1, source_target_pairs={{16,48},{17,49},{18,50},{19,51},{20,52},{21,53},{22,54},{23,55},{2... | collective-permute-start | bytes 3145736 | tf_op jit(solution)/shard_map/ppermute | solution.py:63
  79.9 0.9 copy-start.2
  80.7 6.8 %copy-start.8 = (f32[1024]{0:T(1024)S(1)}, f32[1024]{0:T(1024)}, u32[]{:S(2)}) copy-start(f32[1024]{0:T(1024)} %param.13) | copy-start | bytes 12292
  80.7 25.8 %all-to-all-start = ((bf16[16,32,768]{2,1,0:T(8,128)(2,1)}), bf16[16,32,768]{2,1,0:T(8,128)(2,1)}, u32[]{:S(2)}, u32[]{:S(2)}) async-start(bf16[16,32,768]{2,1,0:T(8,128)(2,1)} %copy-done.2), calls=%async_computation | async-start | bytes 1572864 | tf_op jit(solution)/shard_map/all_to_all | solution.py:322
  99.3 0.7 copy-start.4
  106.6 13.7 %copy-start.5 = (f32[256,256]{1,0:T(8,128)S(1)}, f32[256,256]{1,0:T(8,128)}, u32[]{:S(2)}) copy-start(f32[256,256]{1,0:T(8,128)} %copy-done.4) | copy-start | bytes 786436
  108.0 5.5 %collective-permute-start.14 = (f32[32,256]{1,0:T(8,128)S(1)}, f32[32,256]{1,0:T(8,128)S(1)}, u32[]{:S(2)}, u32[]{:S(2)}) collective-permute-start(f32[32,256]{1,0:T(8,128)S(1)} %pad_maximum_fusion), channel_id=1, source_target_pairs={{0,32},{1,33},{2,34},{3,35},{4,36},{5,37},{6,38},{7,39},{8,40},{9,... | collective-permute-start | bytes 98312 | tf_op jit(solution)/shard_map/ppermute | solution.py:63
  111.9 7.5 %collective-permute-start.15 = (f32[32,128]{1,0:T(8,128)S(1)}, f32[32,128]{1,0:T(8,128)S(1)}, u32[]{:S(2)}, u32[]{:S(2)}) collective-permute-start(f32[32,128]{1,0:T(8,128)S(1)} %get-tuple-element.11), channel_id=1, source_target_pairs={{0,64},{1,65},{2,66},{3,67},{4,68},{5,69},{6,70},{7,71},{8,72},{9,... | collective-permute-start | bytes 49160 | tf_op jit(solution)/shard_map/ppermute | solution.py:63
  120.1 2.0 %collective-permute-start.16 = (f32[256,512]{1,0:T(8,128)S(1)}, f32[256,512]{1,0:T(8,128)S(1)}, u32[]{:S(2)}, u32[]{:S(2)}) collective-permute-start(f32[256,512]{1,0:T(8,128)S(1)} %convolution_subtract_fusion), channel_id=1, source_target_pairs={{0,16},{1,17},{2,18},{3,19},{4,20},{5,21},{6,22},{7,23},{8,24},{9,... | collective-permute-start | bytes 1572872 | tf_op jit(solution)/shard_map/ppermute | solution.py:63
  122.8 7.9 %collective-permute-start.17 = (f32[64,512]{1,0:T(8,128)S(1)}, f32[64,512]{1,0:T(8,128)S(1)}, u32[]{:S(2)}, u32[]{:S(2)}) collective-permute-start(f32[64,512]{1,0:T(8,128)S(1)} %get-tuple-element.18), channel_id=1, source_target_pairs={{0,8},{1,9},{2,10},{3,11},{4,12},{5,13},{6,14},{7,15},{8,0},{9,1},... | collective-permute-start | bytes 393224 | tf_op jit(solution)/shard_map/ppermute | solution.py:63
  125.1 7.6 %collective-permute-start.18 = (f32[64,512]{1,0:T(8,128)S(1)}, f32[64,512]{1,0:T(8,128)S(1)}, u32[]{:S(2)}, u32[]{:S(2)}) collective-permute-start(f32[64,512]{1,0:T(8,128)S(1)} %get-tuple-element.20), channel_id=1, source_target_pairs={{0,4},{1,5},{2,6},{3,7},{4,8},{5,9},{6,10},{7,11},{8,12},{9,13},{1... | collective-permute-start | bytes 393224 | tf_op jit(solution)/shard_map/ppermute | solution.py:63
  125.7 7.0 %collective-permute-start.19 = (f32[64,512]{1,0:T(8,128)S(1)}, f32[64,512]{1,0:T(8,128)S(1)}, u32[]{:S(2)}, u32[]{:S(2)}) collective-permute-start(f32[64,512]{1,0:T(8,128)S(1)} %get-tuple-element.19), channel_id=1, source_target_pairs={{0,12},{1,13},{2,14},{3,15},{4,0},{5,1},{6,2},{7,3},{8,4},{9,5},{1... | collective-permute-start | bytes 393224 | tf_op jit(solution)/shard_map/ppermute | solution.py:63
  132.8 6.6 %collective-permute-start.20 = (f32[16,512]{1,0:T(8,128)S(1)}, f32[16,512]{1,0:T(8,128)S(1)}, u32[]{:S(2)}, u32[]{:S(2)}) collective-permute-start(f32[16,512]{1,0:T(8,128)S(1)} %get-tuple-element.25), channel_id=1, source_target_pairs={{0,2},{1,3},{2,0},{3,1},{4,6},{5,7},{6,4},{7,5},{8,10},{9,11},{10,... | collective-permute-start | bytes 98312 | tf_op jit(solution)/shard_map/ppermute | solution.py:63
  135.6 5.7 %collective-permute-start.21 = (f32[16,512]{1,0:T(8,128)S(1)}, f32[16,512]{1,0:T(8,128)S(1)}, u32[]{:S(2)}, u32[]{:S(2)}) collective-permute-start(f32[16,512]{1,0:T(8,128)S(1)} %get-tuple-element.27), channel_id=1, source_target_pairs={{0,1},{1,2},{2,3},{3,0},{4,5},{5,6},{6,7},{7,4},{8,9},{9,10},{10,1... | collective-permute-start | bytes 98312 | tf_op jit(solution)/shard_map/ppermute | solution.py:63
  135.8 5.5 %collective-permute-start.22 = (f32[16,512]{1,0:T(8,128)S(1)}, f32[16,512]{1,0:T(8,128)S(1)}, u32[]{:S(2)}, u32[]{:S(2)}) collective-permute-start(f32[16,512]{1,0:T(8,128)S(1)} %get-tuple-element.26), channel_id=1, source_target_pairs={{0,3},{1,0},{2,1},{3,2},{4,7},{5,4},{6,5},{7,6},{8,11},{9,8},{10,9... | collective-permute-start | bytes 98312 | tf_op jit(solution)/shard_map/ppermute | solution.py:63

commit v3 on v2

--- a/solution.py
+++ b/solution.py
@@ -294,7 +294,9 @@
     opposite = permute(above, Y_DOWN)
     near = [own, above, opposite, below]
 
-    block = pick_rows(group_order, queries)
+    slot = jnp.arange(qc, dtype=jnp.int32)
+    pick = (group_order[0][:, None] == slot[None, :]).astype(bf16)
+    block = jnp.dot(pick, queries, preferred_element_type=jnp.float32).astype(bf16)
     up1 = permute(block, ODD_UP)
     block_o = permute(block, CORE)
     row = jnp.arange(256, dtype=jnp.int32)
@@ -315,7 +317,7 @@
     bottom = y == 0
     cross = permute(hold(jnp.where(bottom, up1, block), far_own), CROSS)
     even_on = permute(hold(block, far_opposite), EVEN_UP)
-    odd_on = permute(hold(up1, far_opposite), ODD_AGAIN)
+    odd_on = permute(up1, ODD_AGAIN)
     crossed = permute(cross, CROSSED_ON)
 
     sent = products(z.reshape(1), order, near, far, others)

time: 143 us -> 143 us (level)
  waiting for transfers between devices: 54.6 us -> 61.1 us
  starting transfers between devices: 53.2 us -> 47.3 us
  Pallas kernels: 17.4 us -> 19.8 us
  local copies, waits for them, and re-layouts: 12.2 us -> 9.89 us
    ppermute x23, starting transfers between devices: 47.2 us -> 41.5 us  [permute(): return lax.ppermute(value, BOTH, pairs)]
    ppermute x23, waiting for transfers between devices: 48 us -> 51.6 us  [permute(): return lax.ppermute(value, BOTH, pairs)]
    all_to_all x1, waiting for transfers between devices: 6.59 us -> 9.58 us  [per_device(): got = lax.all_to_all(sent, 'feat', 0, 0)]
    unnamed x20 -> x23, local copies, waits for them, and re-layouts: 10.2 us -> 7.83 us
  transfers between devices with their start and end apart: 24 -> 24, of which waited for: 12 -> 13; matrix products, arithmetic and copies ran while one was open for 4% -> 3% of each run, Pallas kernels for 12% -> 14%
where the time goes in v3:
time: 143 us; the launch traced here: 142 us
  waiting for transfers between devices  61.1 us (43%)
  starting transfers between devices  47.3 us (33%)
  Pallas kernels  19.8 us (14%)
  local copies, waits for them, and re-layouts  9.89 us (7%)
  matrix products  2.38 us (2%)
  other arithmetic  1.59 us (1%)
    ppermute x23, waiting for transfers between devices, permute(): return lax.ppermute(value, BOTH, pairs)  51.6 us
    ppermute x23, starting transfers between devices, permute(): return lax.ppermute(value, BOTH, pairs)  41.5 us
    all_to_all x1, waiting for transfers between devices, per_device(): got = lax.all_to_all(sent, 'feat', 0, 0)  9.58 us
    unnamed x23, local copies, waits for them, and re-layouts  7.83 us
    pallas_call x1, Pallas kernels, products(): pl.pallas_call(products_kernel, out_shape=jax.ShapeDtypeStruct((16, 2 * n...  7.81 us
    pallas_call x1, Pallas kernels, sum_docs(): pl.pallas_call(docs_kernel, out_shape=jax.ShapeDtypeStruct((DOC_DEV, widt...  6.43 us
    all_to_all x1, starting transfers between devices, per_device(): got = lax.all_to_all(sent, 'feat', 0, 0)  5.83 us
    pallas_call x1, Pallas kernels, direct_products(): pl.pallas_call(direct_kernel, out_shape=[jax.ShapeDtypeStruct((DOC_DEV, 2...  5.57 us
  transfers between devices with their start and end apart: 24, of which 13 were waited for; matrix products, arithmetic and copies ran while one was open for 3% of the time, Pallas kernels for 14%

profile of v3, /device:TPU:8, one launch (start us, length us, event | category | flops | bytes accessed | tf_op | source)
XLA Modules:
  0.0 142.5 jit_solution(9963021899669631038)
XLA Ops:
  0.0 1.2 copy-done
  1.2 1.1 convolution_convert_fusion.q_ref.refs_8_
  2.4 1.7 %collective-permute-start.1 = (bf16[128,4096]{1,0:T(8,128)(2,1)S(1)}, bf16[128,4096]{1,0:T(8,128)(2,1)}, u32[]{:S(2)}, u32[]{:S(2)}) collective-permute-start(bf16[128,4096]{1,0:T(8,128)(2,1)S(1)} %convolution_convert_fusion.q_ref.refs_8_), channel_id=1, source_target_pairs={{16,48},{17,49},{18,50},{19,51},{20,52},{21,53},{22,54},{23,55},{2... | collective-permute-start | bytes 3145736 | tf_op jit(solution)/shard_map/ppermute | solution.py:63
  4.0 2.2 %collective-permute-start.4 = (bf16[64,4096]{1,0:T(8,128)(2,1)}, bf16[64,4096]{1,0:T(8,128)(2,1)}, u32[]{:S(2)}, u32[]{:S(2)}) collective-permute-start(bf16[64,4096]{1,0:T(8,128)(2,1)} %refs_0_.1), channel_id=1, source_target_pairs={{0,96},{1,97},{2,98},{3,99},{4,100},{5,101},{6,102},{7,103},{8,104... | collective-permute-start | bytes 1572872 | tf_op jit(solution)/shard_map/ppermute | solution.py:63
  6.2 7.0 %collective-permute-start.2 = (bf16[64,4096]{1,0:T(8,128)(2,1)}, bf16[64,4096]{1,0:T(8,128)(2,1)S(1)}, u32[]{:S(2)}, u32[]{:S(2)}) collective-permute-start(bf16[64,4096]{1,0:T(8,128)(2,1)} %refs_0_.1), channel_id=1, source_target_pairs={{0,128},{1,129},{2,130},{3,131},{4,132},{5,133},{6,134},{7,135},{8... | collective-permute-start | bytes 1572872 | tf_op jit(solution)/shard_map/ppermute | solution.py:63
  13.3 0.6 collective-permute-start.13
  13.9 3.4 %copy-done.1 = bf16[1024,4096]{1,0:T(8,128)(2,1)S(1)} copy-done((bf16[1024,4096]{1,0:T(8,128)(2,1)S(1)}, bf16[1024,4096]{1,0:T(8,128)(2,1)}, u32[]{:S(2)}) %copy-start.1) | copy-done | bytes 8388632
  17.3 6.4 %sum_docs.1.d_ref.refs_9_ = bf16[256,4096]{1,0:T(8,128)(2,1)} custom-call(s32[1,1024]{1,0:T(1,128)S(1)} %copy-done.8, bf16[1024,4096]{1,0:T(8,128)(2,1)S(1)} %copy-done.1), custom_call_target="tpu_custom_call" | custom-call | tf_op jit(solution)/shard_map/sum_docs/pallas_call | solution.py:140
  23.7 0.1 collective-permute-start
  23.8 1.3 collective-permute-start.5
  25.1 1.1 broadcast_select_fusion.refs_0_
  26.2 0.0 collective-permute-done.3.refs_1_.refs_3_
  26.2 10.3 %collective-permute-done.2.refs_0_ = bf16[64,4096]{1,0:T(8,128)(2,1)S(1)} collective-permute-done((bf16[64,4096]{1,0:T(8,128)(2,1)}, bf16[64,4096]{1,0:T(8,128)(2,1)S(1)}, u32[]{:S(2)}, u32[]{:S(2)}) %collective-permute-start.2) | collective-permute-done | bytes 524320 | tf_op jit(solution)/shard_map/ppermute | solution.py:63
  36.6 1.9 %collective-permute-done.5.refs_2_ = bf16[64,4096]{1,0:T(8,128)(2,1)} collective-permute-done((bf16[64,4096]{1,0:T(8,128)(2,1)}, bf16[64,4096]{1,0:T(8,128)(2,1)}, u32[]{:S(2)}, u32[]{:S(2)}) %collective-permute-start.5) | collective-permute-done | bytes 524320 | tf_op jit(solution)/shard_map/ppermute | solution.py:63
  38.5 1.8 %collective-permute-start.6 = (bf16[128,4096]{1,0:T(8,128)(2,1)}, bf16[128,4096]{1,0:T(8,128)(2,1)}, u32[]{:S(2)}, u32[]{:S(2)}) collective-permute-start(bf16[128,4096]{1,0:T(8,128)(2,1)} %hold.4), channel_id=1, source_target_pairs={{16,144},{17,145},{18,146},{19,147},{20,148},{21,149},{22,150},{23... | collective-permute-start | bytes 3145736 | tf_op jit(solution)/shard_map/ppermute | solution.py:63
  40.3 7.6 %collective-permute-start.7 = (bf16[64,4096]{1,0:T(8,128)(2,1)S(1)}, bf16[64,4096]{1,0:T(8,128)(2,1)S(1)}, u32[]{:S(2)}, u32[]{:S(2)}) collective-permute-start(bf16[64,4096]{1,0:T(8,128)(2,1)S(1)} %copy-done.3), channel_id=1, source_target_pairs={{0,64},{1,65},{2,66},{3,67},{4,68},{5,69},{6,70},{7,71},{8,72},{9,... | collective-permute-start | bytes 1572872 | tf_op jit(solution)/shard_map/ppermute | solution.py:63
  47.9 0.0 collective-permute-start.11
  47.9 12.8 %collective-permute-done.7.refs_1_.refs_6_ = bf16[64,4096]{1,0:T(8,128)(2,1)S(1)} collective-permute-done((bf16[64,4096]{1,0:T(8,128)(2,1)S(1)}, bf16[64,4096]{1,0:T(8,128)(2,1)S(1)}, u32[]{:S(2)}, u32[]{:S(2)}) %collective-permute-start.7) | collective-permute-done | bytes 524320 | tf_op jit(solution)/shard_map/ppermute | solution.py:63
  60.7 0.0 collective-permute-start.12
  60.7 1.0 copy.13.refs_0_
  61.7 0.1 copy-done.4
  61.8 0.0 collective-permute-done.13.refs_10_
  61.9 1.6 %collective-permute-start.9 = (bf16[128,4096]{1,0:T(8,128)(2,1)}, bf16[128,4096]{1,0:T(8,128)(2,1)}, u32[]{:S(2)}, u32[]{:S(2)}) collective-permute-start(bf16[128,4096]{1,0:T(8,128)(2,1)} %collective-permute-done.1.up1), channel_id=1, source_target_pairs={{48,80},{49,81},{50,82},{51,83},{52,84},{53,85},{54,86},{55,87},{5... | collective-permute-start | bytes 3145736 | tf_op jit(solution)/shard_map/ppermute | solution.py:63
  63.5 3.7 %collective-permute-done.11.refs_5_ = bf16[64,4096]{1,0:T(8,128)(2,1)} collective-permute-done((bf16[64,4096]{1,0:T(8,128)(2,1)S(1)}, bf16[64,4096]{1,0:T(8,128)(2,1)}, u32[]{:S(2)}, u32[]{:S(2)}) %collective-permute-start.11) | collective-permute-done | bytes 524320 | tf_op jit(solution)/shard_map/ppermute | solution.py:63
  67.2 2.5 %collective-permute-start.8 = (bf16[128,4096]{1,0:T(8,128)(2,1)}, bf16[128,4096]{1,0:T(8,128)(2,1)}, u32[]{:S(2)}, u32[]{:S(2)}) collective-permute-start(bf16[128,4096]{1,0:T(8,128)(2,1)} %hold.5), channel_id=1, source_target_pairs={{0,32},{1,33},{2,34},{3,35},{4,36},{5,37},{6,38},{7,39},{8,40},{9,... | collective-permute-start | bytes 3145736 | tf_op jit(solution)/shard_map/ppermute | solution.py:63
  69.7 0.0 collective-permute-done.6.cross
  69.7 1.7 %collective-permute-start.10 = (bf16[128,4096]{1,0:T(8,128)(2,1)}, bf16[128,4096]{1,0:T(8,128)(2,1)}, u32[]{:S(2)}, u32[]{:S(2)}) collective-permute-start(bf16[128,4096]{1,0:T(8,128)(2,1)} %collective-permute-done.6.cross), channel_id=1, source_target_pairs={{16,48},{17,49},{18,50},{19,51},{20,52},{21,53},{22,54},{23,55},{2... | collective-permute-start | bytes 3145736 | tf_op jit(solution)/shard_map/ppermute | solution.py:63
  71.4 0.1 fusion.1.order_ref
  71.5 1.6 %collective-permute-done.12.refs_7_ = bf16[64,4096]{1,0:T(8,128)(2,1)} collective-permute-done((bf16[64,4096]{1,0:T(8,128)(2,1)S(1)}, bf16[64,4096]{1,0:T(8,128)(2,1)}, u32[]{:S(2)}, u32[]{:S(2)}) %collective-permute-start.12) | collective-permute-done | bytes 524320 | tf_op jit(solution)/shard_map/ppermute | solution.py:63
  73.1 0.0 collective-permute-done.do_ref.refs_11_
  73.1 1.0 copy-done.5
  74.1 1.0 copy-done.7
  75.2 7.8 %products.1 = bf16[16,32,768]{2,1,0:T(8,128)(2,1)} custom-call(s32[1]{0:T(128)} %bitcast.3.flag, bf16[256,256]{1,0:T(8,128)(2,1)S(1)} %fusion.1.order_ref, bf16[64,4096]{1,0:T(8,128)(2,1)} %refs_0_.1, bf16[64,4096]{1,0:T(8,128)(2,1)} %collective-permute-done.4.refs_1_, bf16[64,4096]{1,0:T(8,128)(2,1)} %collective-permute-done.5.refs_2_, ...), custom_call_target="tpu_custom_call" | custom-call | tf_op jit(solution)/shard_map/products/pallas_call | solution.py:199
  83.0 0.0 copy-start.10
  83.0 5.8 %all-to-all-start = ((bf16[16,32,768]{2,1,0:T(8,128)(2,1)}), bf16[16,32,768]{2,1,0:T(8,128)(2,1)S(1)}, u32[]{:S(2)}, u32[]{:S(2)}) async-start(bf16[16,32,768]{2,1,0:T(8,128)(2,1)} %products.1), calls=%async_computation | async-start | bytes 1572864 | tf_op jit(solution)/shard_map/all_to_all | solution.py:324
  88.9 0.7 gather_fusion
  89.6 0.7 gather_fusion.1
  90.3 0.1 pad_add_fusion.flags
  90.3 0.0 collective-permute-done.9.odd
  90.4 4.4 %collective-permute-done.8.even = bf16[128,4096]{1,0:T(8,128)(2,1)} collective-permute-done((bf16[128,4096]{1,0:T(8,128)(2,1)}, bf16[128,4096]{1,0:T(8,128)(2,1)}, u32[]{:S(2)}, u32[]{:S(2)}) %collective-permute-start.8) | collective-permute-done | bytes 1048608 | tf_op jit(solution)/shard_map/ppermute | solution.py:63
  94.8 0.0 collective-permute-done.10.on
  94.8 5.6 %direct_products.1 = (f32[256,256]{1,0:T(8,128)S(1)}, f32[256,384]{1,0:T(8,128)S(1)}) custom-call(s32[2]{0:T(128)S(1)} %pad_add_fusion.flags, bf16[256,4096]{1,0:T(8,128)(2,1)} %sum_docs.1.d_ref.refs_9_, bf16[256,4096]{1,0:T(8,128)(2,1)} %collective-permute-done.do_ref.refs_11_, bf16[128,4096]{1,0:T(8,128)(2,1)S(1)} %convolution_convert_fusion.q_ref.refs_8_, ...), custom_call_target="tpu_custom_call" | custom-call | flops 6710886400 | bytes 10485760 | tf_op jit(solution)/shard_map/direct_products/pallas_call | solution.py:237
  100.4 9.6 %all-to-all-done = bf16[16,32,768]{2,1,0:T(8,128)(2,1)S(1)} async-done(((bf16[16,32,768]{2,1,0:T(8,128)(2,1)}), bf16[16,32,768]{2,1,0:T(8,128)(2,1)S(1)}, u32[]{:S(2)}, u32[]{:S(2)}) %all-to-all-start) | async-done | bytes 786464 | tf_op jit(solution)/shard_map/all_to_all | solution.py:324
  110.0 0.1 convert_reduce_fusion
  110.1 0.1 broadcast_select_fusion.8
  110.1 3.5 %collective-permute-start.14 = (f32[32,256]{1,0:T(8,128)S(1)}, f32[32,256]{1,0:T(8,128)S(1)}, u32[]{:S(2)}, u32[]{:S(2)}) collective-permute-start(f32[32,256]{1,0:T(8,128)S(1)} %pad_maximum_fusion), channel_id=1, source_target_pairs={{0,32},{1,33},{2,34},{3,35},{4,36},{5,37},{6,38},{7,39},{8,40},{9,... | collective-permute-start | bytes 98312 | tf_op jit(solution)/shard_map/ppermute | solution.py:63
  113.6 0.1 collective-permute-start.15
  113.8 1.4 %collective-permute-done.14 = f32[32,256]{1,0:T(8,128)S(1)} collective-permute-done((f32[32,256]{1,0:T(8,128)S(1)}, f32[32,256]{1,0:T(8,128)S(1)}, u32[]{:S(2)}, u32[]{:S(2)}) %collective-permute-start.14) | collective-permute-done | bytes 32800 | tf_op jit(solution)/shard_map/ppermute | solution.py:63
  115.2 5.8 %collective-permute-done.15 = f32[32,128]{1,0:T(8,128)S(1)} collective-permute-done((f32[32,128]{1,0:T(8,128)S(1)}, f32[32,128]{1,0:T(8,128)S(1)}, u32[]{:S(2)}, u32[]{:S(2)}) %collective-permute-start.15) | collective-permute-done | bytes 16416 | tf_op jit(solution)/shard_map/ppermute | solution.py:63
  121.1 0.6 convolution_subtract_fusion
  121.7 0.1 collective-permute-start.16
  121.9 1.8 %collective-permute-done.16 = f32[256,512]{1,0:T(8,128)S(1)} collective-permute-done((f32[256,512]{1,0:T(8,128)S(1)}, f32[256,512]{1,0:T(8,128)S(1)}, u32[]{:S(2)}, u32[]{:S(2)}) %collective-permute-start.16) | collective-permute-done | bytes 524320 | tf_op jit(solution)/shard_map/ppermute | solution.py:63
  123.7 0.6 fusion
  124.4 0.9 collective-permute-start.17
  125.4 1.0 collective-permute-start.18
  126.4 2.2 %collective-permute-start.19 = (f32[64,512]{1,0:T(8,128)S(1)}, f32[64,512]{1,0:T(8,128)S(1)}, u32[]{:S(2)}, u32[]{:S(2)}) collective-permute-start(f32[64,512]{1,0:T(8,128)S(1)} %get-tuple-element.19), channel_id=1, source_target_pairs={{0,12},{1,13},{2,14},{3,15},{4,0},{5,1},{6,2},{7,3},{8,4},{9,5},{1... | collective-permute-start | bytes 393224 | tf_op jit(solution)/shard_map/ppermute | solution.py:63
  128.6 3.8 %collective-permute-done.17 = f32[64,512]{1,0:T(8,128)S(1)} collective-permute-done((f32[64,512]{1,0:T(8,128)S(1)}, f32[64,512]{1,0:T(8,128)S(1)}, u32[]{:S(2)}, u32[]{:S(2)}) %collective-permute-start.17) | collective-permute-done | bytes 131104 | tf_op jit(solution)/shard_map/ppermute | solution.py:63
  132.4 2.0 %collective-permute-done.18 = f32[64,512]{1,0:T(8,128)S(1)} collective-permute-done((f32[64,512]{1,0:T(8,128)S(1)}, f32[64,512]{1,0:T(8,128)S(1)}, u32[]{:S(2)}, u32[]{:S(2)}) %collective-permute-start.18) | collective-permute-done | bytes 131104 | tf_op jit(solution)/shard_map/ppermute | solution.py:63
  134.4 1.7 %collective-permute-start.20 = (f32[16,512]{1,0:T(8,128)S(1)}, f32[16,512]{1,0:T(8,128)S(1)}, u32[]{:S(2)}, u32[]{:S(2)}) collective-permute-start(f32[16,512]{1,0:T(8,128)S(1)} %get-tuple-element.25), channel_id=1, source_target_pairs={{0,2},{1,3},{2,0},{3,1},{4,6},{5,7},{6,4},{7,5},{8,10},{9,11},{10,... | collective-permute-start | bytes 98312 | tf_op jit(solution)/shard_map/ppermute | solution.py:63
  136.1 0.0 collective-permute-start.21
  136.1 3.8 %collective-permute-start.22 = (f32[16,512]{1,0:T(8,128)S(1)}, f32[16,512]{1,0:T(8,128)S(1)}, u32[]{:S(2)}, u32[]{:S(2)}) collective-permute-start(f32[16,512]{1,0:T(8,128)S(1)} %get-tuple-element.26), channel_id=1, source_target_pairs={{0,3},{1,0},{2,1},{3,2},{4,7},{5,4},{6,5},{7,6},{8,11},{9,8},{10,9... | collective-permute-start | bytes 98312 | tf_op jit(solution)/shard_map/ppermute | solution.py:63
  139.9 1.9 %collective-permute-done.21 = f32[16,512]{1,0:T(8,128)S(1)} collective-permute-done((f32[16,512]{1,0:T(8,128)S(1)}, f32[16,512]{1,0:T(8,128)S(1)}, u32[]{:S(2)}, u32[]{:S(2)}) %collective-permute-start.21) | collective-permute-done | bytes 32800 | tf_op jit(solution)/shard_map/ppermute | solution.py:63
  141.8 0.0 collective-permute-done.22
  141.8 0.6 reshape.153
  (39 shorter events, 0.3 us)
Async XLA Ops:
  0.0 1.2 copy-start
  0.0 13.9 %copy-start.8 = (s32[1,1024]{1,0:T(1,128)S(1)}, s32[1,1024]{1,0:T(1,128)}, u32[]{:S(2)}) copy-start(s32[1,1024]{1,0:T(1,128)} %ids_ref.1) | copy-start | bytes 12292
  2.4 21.4 %collective-permute-start.1 = (bf16[128,4096]{1,0:T(8,128)(2,1)S(1)}, bf16[128,4096]{1,0:T(8,128)(2,1)}, u32[]{:S(2)}, u32[]{:S(2)}) collective-permute-start(bf16[128,4096]{1,0:T(8,128)(2,1)S(1)} %convolution_convert_fusion.q_ref.refs_8_), channel_id=1, source_target_pairs={{16,48},{17,49},{18,50},{19,51},{20,52},{21,53},{22,54},{23,55},{2... | collective-permute-start | bytes 3145736 | tf_op jit(solution)/shard_map/ppermute | solution.py:63
  4.0 19.6 %collective-permute-start.4 = (bf16[64,4096]{1,0:T(8,128)(2,1)}, bf16[64,4096]{1,0:T(8,128)(2,1)}, u32[]{:S(2)}, u32[]{:S(2)}) collective-permute-start(bf16[64,4096]{1,0:T(8,128)(2,1)} %refs_0_.1), channel_id=1, source_target_pairs={{0,96},{1,97},{2,98},{3,99},{4,100},{5,101},{6,102},{7,103},{8,104... | collective-permute-start | bytes 1572872 | tf_op jit(solution)/shard_map/ppermute | solution.py:63
  6.2 20.0 %collective-permute-start.3 = (bf16[64,4096]{1,0:T(8,128)(2,1)}, bf16[64,4096]{1,0:T(8,128)(2,1)S(1)}, u32[]{:S(2)}, u32[]{:S(2)}) collective-permute-start(bf16[64,4096]{1,0:T(8,128)(2,1)} %refs_0_.1), channel_id=1, source_target_pairs={{0,32},{1,33},{2,34},{3,35},{4,36},{5,37},{6,38},{7,39},{8,40},{9,... | collective-permute-start | bytes 1572872 | tf_op jit(solution)/shard_map/ppermute | solution.py:63
  6.2 30.3 %collective-permute-start.2 = (bf16[64,4096]{1,0:T(8,128)(2,1)}, bf16[64,4096]{1,0:T(8,128)(2,1)S(1)}, u32[]{:S(2)}, u32[]{:S(2)}) collective-permute-start(bf16[64,4096]{1,0:T(8,128)(2,1)} %refs_0_.1), channel_id=1, source_target_pairs={{0,128},{1,129},{2,130},{3,131},{4,132},{5,133},{6,134},{7,135},{8... | collective-permute-start | bytes 1572872 | tf_op jit(solution)/shard_map/ppermute | solution.py:63
  13.3 48.6 %collective-permute-start.13 = (bf16[128,4096]{1,0:T(8,128)(2,1)S(1)}, bf16[128,4096]{1,0:T(8,128)(2,1)}, u32[]{:S(2)}, u32[]{:S(2)}) collective-permute-start(bf16[128,4096]{1,0:T(8,128)(2,1)S(1)} %convolution_convert_fusion.q_ref.refs_8_), channel_id=1, source_target_pairs={{0,16},{1,17},{2,18},{3,19},{4,20},{5,21},{6,22},{7,23},{8,24},{9,... | collective-permute-start | bytes 3145736 | tf_op jit(solution)/shard_map/ppermute | solution.py:63
  13.9 3.4 %copy-start.1 = (bf16[1024,4096]{1,0:T(8,128)(2,1)S(1)}, bf16[1024,4096]{1,0:T(8,128)(2,1)}, u32[]{:S(2)}) copy-start(bf16[1024,4096]{1,0:T(8,128)(2,1)} %rows_ref.1) | copy-start | bytes 25165828
  23.7 49.4 %collective-permute-start = (bf16[256,4096]{1,0:T(8,128)(2,1)}, bf16[256,4096]{1,0:T(8,128)(2,1)}, u32[]{:S(2)}, u32[]{:S(2)}) collective-permute-start(bf16[256,4096]{1,0:T(8,128)(2,1)} %sum_docs.1.d_ref.refs_9_), channel_id=1, source_target_pairs={{0,16},{1,17},{2,18},{3,19},{4,20},{5,21},{6,22},{7,23},{8,24},{9,... | collective-permute-start | bytes 6291464 | tf_op jit(solution)/shard_map/ppermute | solution.py:63
  23.8 14.7 %collective-permute-start.5 = (bf16[64,4096]{1,0:T(8,128)(2,1)}, bf16[64,4096]{1,0:T(8,128)(2,1)}, u32[]{:S(2)}, u32[]{:S(2)}) collective-permute-start(bf16[64,4096]{1,0:T(8,128)(2,1)} %collective-permute-done.4.refs_1_), channel_id=1, source_target_pairs={{0,96},{1,97},{2,98},{3,99},{4,100},{5,101},{6,102},{7,103},{8,104... | collective-permute-start | bytes 1572872 | tf_op jit(solution)/shard_map/ppermute | solution.py:63
  26.2 12.2 %copy-start.6 = (bf16[64,4096]{1,0:T(8,128)(2,1)}, bf16[64,4096]{1,0:T(8,128)(2,1)S(1)}, u32[]{:S(2)}) copy-start(bf16[64,4096]{1,0:T(8,128)(2,1)S(1)} %collective-permute-done.3.refs_1_.refs_3_) | copy-start | bytes 1572868
  36.6 1.9 %copy-start.2 = (bf16[64,4096]{1,0:T(8,128)(2,1)}, bf16[64,4096]{1,0:T(8,128)(2,1)S(1)}, u32[]{:S(2)}) copy-start(bf16[64,4096]{1,0:T(8,128)(2,1)S(1)} %collective-permute-done.2.refs_0_) | copy-start | bytes 1572868
  38.5 1.8 %copy-start.3 = (bf16[64,4096]{1,0:T(8,128)(2,1)S(1)}, bf16[64,4096]{1,0:T(8,128)(2,1)}, u32[]{:S(2)}) copy-start(bf16[64,4096]{1,0:T(8,128)(2,1)} %hold.3.refs_1_.refs_4_) | copy-start | bytes 1572868
  38.5 31.2 %collective-permute-start.6 = (bf16[128,4096]{1,0:T(8,128)(2,1)}, bf16[128,4096]{1,0:T(8,128)(2,1)}, u32[]{:S(2)}, u32[]{:S(2)}) collective-permute-start(bf16[128,4096]{1,0:T(8,128)(2,1)} %hold.4), channel_id=1, source_target_pairs={{16,144},{17,145},{18,146},{19,147},{20,148},{21,149},{22,150},{23... | collective-permute-start | bytes 3145736 | tf_op jit(solution)/shard_map/ppermute | solution.py:63
  40.3 20.4 %collective-permute-start.7 = (bf16[64,4096]{1,0:T(8,128)(2,1)S(1)}, bf16[64,4096]{1,0:T(8,128)(2,1)S(1)}, u32[]{:S(2)}, u32[]{:S(2)}) collective-permute-start(bf16[64,4096]{1,0:T(8,128)(2,1)S(1)} %copy-done.3), channel_id=1, source_target_pairs={{0,64},{1,65},{2,66},{3,67},{4,68},{5,69},{6,70},{7,71},{8,72},{9,... | collective-permute-start | bytes 1572872 | tf_op jit(solution)/shard_map/ppermute | solution.py:63
  47.9 19.3 %collective-permute-start.11 = (bf16[64,4096]{1,0:T(8,128)(2,1)S(1)}, bf16[64,4096]{1,0:T(8,128)(2,1)}, u32[]{:S(2)}, u32[]{:S(2)}) collective-permute-start(bf16[64,4096]{1,0:T(8,128)(2,1)S(1)} %copy-done.3), channel_id=1, source_target_pairs={{0,96},{1,97},{2,98},{3,99},{4,100},{5,101},{6,102},{7,103},{8,104... | collective-permute-start | bytes 1572872 | tf_op jit(solution)/shard_map/ppermute | solution.py:63
  60.7 1.1 copy-start.4
  60.7 12.4 %collective-permute-start.12 = (bf16[64,4096]{1,0:T(8,128)(2,1)S(1)}, bf16[64,4096]{1,0:T(8,128)(2,1)}, u32[]{:S(2)}, u32[]{:S(2)}) collective-permute-start(bf16[64,4096]{1,0:T(8,128)(2,1)S(1)} %copy-done.3), channel_id=1, source_target_pairs={{0,32},{1,33},{2,34},{3,35},{4,36},{5,37},{6,38},{7,39},{8,40},{9,... | collective-permute-start | bytes 1572872 | tf_op jit(solution)/shard_map/ppermute | solution.py:63
  61.9 28.5 %collective-permute-start.9 = (bf16[128,4096]{1,0:T(8,128)(2,1)}, bf16[128,4096]{1,0:T(8,128)(2,1)}, u32[]{:S(2)}, u32[]{:S(2)}) collective-permute-start(bf16[128,4096]{1,0:T(8,128)(2,1)} %collective-permute-done.1.up1), channel_id=1, source_target_pairs={{48,80},{49,81},{50,82},{51,83},{52,84},{53,85},{54,86},{55,87},{5... | collective-permute-start | bytes 3145736 | tf_op jit(solution)/shard_map/ppermute | solution.py:63
  67.2 27.6 %collective-permute-start.8 = (bf16[128,4096]{1,0:T(8,128)(2,1)}, bf16[128,4096]{1,0:T(8,128)(2,1)}, u32[]{:S(2)}, u32[]{:S(2)}) collective-permute-start(bf16[128,4096]{1,0:T(8,128)(2,1)} %hold.5), channel_id=1, source_target_pairs={{0,32},{1,33},{2,34},{3,35},{4,36},{5,37},{6,38},{7,39},{8,40},{9,... | collective-permute-start | bytes 3145736 | tf_op jit(solution)/shard_map/ppermute | solution.py:63
  69.7 25.1 %collective-permute-start.10 = (bf16[128,4096]{1,0:T(8,128)(2,1)}, bf16[128,4096]{1,0:T(8,128)(2,1)}, u32[]{:S(2)}, u32[]{:S(2)}) collective-permute-start(bf16[128,4096]{1,0:T(8,128)(2,1)} %collective-permute-done.6.cross), channel_id=1, source_target_pairs={{16,48},{17,49},{18,50},{19,51},{20,52},{21,53},{22,54},{23,55},{2... | collective-permute-start | bytes 3145736 | tf_op jit(solution)/shard_map/ppermute | solution.py:63
  73.1 1.0 copy-start.5
  74.1 1.0 copy-start.7
  75.2 13.7 %copy-start.9 = (f32[1024]{0:T(1024)S(1)}, f32[1024]{0:T(1024)}, u32[]{:S(2)}) copy-start(f32[1024]{0:T(1024)} %param.12) | copy-start | bytes 12292
  83.0 6.6 %copy-start.10 = (f32[1024]{0:T(1024)S(1)}, f32[1024]{0:T(1024)}, u32[]{:S(2)}) copy-start(f32[1024]{0:T(1024)} %param.13) | copy-start | bytes 12292
  83.0 26.9 %all-to-all-start = ((bf16[16,32,768]{2,1,0:T(8,128)(2,1)}), bf16[16,32,768]{2,1,0:T(8,128)(2,1)S(1)}, u32[]{:S(2)}, u32[]{:S(2)}) async-start(bf16[16,32,768]{2,1,0:T(8,128)(2,1)} %products.1), calls=%async_computation | async-start | bytes 1572864 | tf_op jit(solution)/shard_map/all_to_all | solution.py:324
  110.1 5.1 %collective-permute-start.14 = (f32[32,256]{1,0:T(8,128)S(1)}, f32[32,256]{1,0:T(8,128)S(1)}, u32[]{:S(2)}, u32[]{:S(2)}) collective-permute-start(f32[32,256]{1,0:T(8,128)S(1)} %pad_maximum_fusion), channel_id=1, source_target_pairs={{0,32},{1,33},{2,34},{3,35},{4,36},{5,37},{6,38},{7,39},{8,40},{9,... | collective-permute-start | bytes 98312 | tf_op jit(solution)/shard_map/ppermute | solution.py:63
  113.6 7.4 %collective-permute-start.15 = (f32[32,128]{1,0:T(8,128)S(1)}, f32[32,128]{1,0:T(8,128)S(1)}, u32[]{:S(2)}, u32[]{:S(2)}) collective-permute-start(f32[32,128]{1,0:T(8,128)S(1)} %get-tuple-element.11), channel_id=1, source_target_pairs={{0,64},{1,65},{2,66},{3,67},{4,68},{5,69},{6,70},{7,71},{8,72},{9,... | collective-permute-start | bytes 49160 | tf_op jit(solution)/shard_map/ppermute | solution.py:63
  121.7 2.0 %collective-permute-start.16 = (f32[256,512]{1,0:T(8,128)S(1)}, f32[256,512]{1,0:T(8,128)S(1)}, u32[]{:S(2)}, u32[]{:S(2)}) collective-permute-start(f32[256,512]{1,0:T(8,128)S(1)} %convolution_subtract_fusion), channel_id=1, source_target_pairs={{0,16},{1,17},{2,18},{3,19},{4,20},{5,21},{6,22},{7,23},{8,24},{9,... | collective-permute-start | bytes 1572872 | tf_op jit(solution)/shard_map/ppermute | solution.py:63
  124.4 8.0 %collective-permute-start.17 = (f32[64,512]{1,0:T(8,128)S(1)}, f32[64,512]{1,0:T(8,128)S(1)}, u32[]{:S(2)}, u32[]{:S(2)}) collective-permute-start(f32[64,512]{1,0:T(8,128)S(1)} %get-tuple-element.18), channel_id=1, source_target_pairs={{0,8},{1,9},{2,10},{3,11},{4,12},{5,13},{6,14},{7,15},{8,0},{9,1},... | collective-permute-start | bytes 393224 | tf_op jit(solution)/shard_map/ppermute | solution.py:63
  125.4 9.0 %collective-permute-start.18 = (f32[64,512]{1,0:T(8,128)S(1)}, f32[64,512]{1,0:T(8,128)S(1)}, u32[]{:S(2)}, u32[]{:S(2)}) collective-permute-start(f32[64,512]{1,0:T(8,128)S(1)} %get-tuple-element.20), channel_id=1, source_target_pairs={{0,4},{1,5},{2,6},{3,7},{4,8},{5,9},{6,10},{7,11},{8,12},{9,13},{1... | collective-permute-start | bytes 393224 | tf_op jit(solution)/shard_map/ppermute | solution.py:63
  126.4 8.0 %collective-permute-start.19 = (f32[64,512]{1,0:T(8,128)S(1)}, f32[64,512]{1,0:T(8,128)S(1)}, u32[]{:S(2)}, u32[]{:S(2)}) collective-permute-start(f32[64,512]{1,0:T(8,128)S(1)} %get-tuple-element.19), channel_id=1, source_target_pairs={{0,12},{1,13},{2,14},{3,15},{4,0},{5,1},{6,2},{7,3},{8,4},{9,5},{1... | collective-permute-start | bytes 393224 | tf_op jit(solution)/shard_map/ppermute | solution.py:63
  134.4 5.5 %collective-permute-start.20 = (f32[16,512]{1,0:T(8,128)S(1)}, f32[16,512]{1,0:T(8,128)S(1)}, u32[]{:S(2)}, u32[]{:S(2)}) collective-permute-start(f32[16,512]{1,0:T(8,128)S(1)} %get-tuple-element.25), channel_id=1, source_target_pairs={{0,2},{1,3},{2,0},{3,1},{4,6},{5,7},{6,4},{7,5},{8,10},{9,11},{10,... | collective-permute-start | bytes 98312 | tf_op jit(solution)/shard_map/ppermute | solution.py:63
  136.1 5.7 %collective-permute-start.21 = (f32[16,512]{1,0:T(8,128)S(1)}, f32[16,512]{1,0:T(8,128)S(1)}, u32[]{:S(2)}, u32[]{:S(2)}) collective-permute-start(f32[16,512]{1,0:T(8,128)S(1)} %get-tuple-element.27), channel_id=1, source_target_pairs={{0,1},{1,2},{2,3},{3,0},{4,5},{5,6},{6,7},{7,4},{8,9},{9,10},{10,1... | collective-permute-start | bytes 98312 | tf_op jit(solution)/shard_map/ppermute | solution.py:63
  136.1 5.7 %collective-permute-start.22 = (f32[16,512]{1,0:T(8,128)S(1)}, f32[16,512]{1,0:T(8,128)S(1)}, u32[]{:S(2)}, u32[]{:S(2)}) collective-permute-start(f32[16,512]{1,0:T(8,128)S(1)} %get-tuple-element.26), channel_id=1, source_target_pairs={{0,3},{1,0},{2,1},{3,2},{4,7},{5,4},{6,5},{7,6},{8,11},{9,8},{10,9... | collective-permute-start | bytes 98312 | tf_op jit(solution)/shard_map/ppermute | solution.py:63
